TPU v7x, 128 devices: a whole 4x4x4 slice. The times are simulated.
128 devices in a mesh: prompt: 8 (over x, y_hi), resp: 16 (over z, y_lo, core).
Axes of the slice: x: 4, y: 4 (y_hi: 2, y_lo: 2; y = y_hi * 2 + y_lo), z: 4, core: 2. Of those that a mesh axis runs over, the one named last changes fastest.
Arguments:
- queries: bfloat16 [8, 16, 128, 8192], P('prompt', 'resp'), may hold values from -100 to 100
- response_key_rows: bfloat16 [8, 16, 128, 1024], P('prompt', 'resp'), may hold values from -5 to 5
- response_value_rows: bfloat16 [8, 16, 128, 1024], P('prompt', 'resp'), may hold values from -5 to 5
- prompt_keys: bfloat16 [8, 1024, 1024], P('prompt', 'resp'), may hold values from -6 to 6
- prompt_value_rows: bfloat16 [8, 1024, 1024], P('prompt', 'resp'), may hold values from -5 to 5
- out_grad: bfloat16 [8, 16, 128, 8192], P('prompt', 'resp'), may hold values from -5 to 5
- resp_lengths: int32 [8, 16], P('prompt', 'resp'), may hold values from 1 to 128, as said below
Outputs:
- attended: bfloat16 [8, 16, 128, 8192], P('prompt', 'resp')
- query_grad: bfloat16 [8, 16, 128, 8192], P('prompt', 'resp')
- resp_key_grad: bfloat16 [8, 16, 128, 1024], P('prompt', 'resp')
- resp_value_grad: bfloat16 [8, 16, 128, 1024], P('prompt', 'resp')
- prompt_key_grad: bfloat16 [8, 1024, 1024], P('prompt', 'resp')
- prompt_value_grad: bfloat16 [8, 1024, 1024], P('prompt', 'resp')
Inputs may be any that keep to these rules, and one draw needn't show every extreme that they name: `resp_lengths`: one response in every draw has all 128 tokens live.
All inputs are finite; a program needn't handle non-finite values.
Results may differ from a plain program's by a relative error of at most 0.015.
Values may be sent and summed in bfloat16 or wider, within the bound.
A program may use at most 128 MiB of HBM per device.

v0:
```python
import jax
import jax.numpy as jnp
from jax import lax
from jax.sharding import PartitionSpec as P

QUERY_HEADS = 64
KEY_VALUE_HEADS = 8
HEAD_DIM = 128


def response_pass(
    queries,
    response_key_block,
    response_value_block,
    prompt_key_rows,
    prompt_value_block,
    grads,
    live,
    factor,
):
    row_count = queries.shape[0]
    plen = prompt_key_rows.shape[0]
    key_total_count = plen + row_count
    group_index = QUERY_HEADS // KEY_VALUE_HEADS
    inv = 1.0 / HEAD_DIM**0.5
    key_rows = (
        jnp.concatenate([prompt_key_rows, response_key_block], 0)
        .reshape(key_total_count, KEY_VALUE_HEADS, HEAD_DIM)
        .transpose(1, 0, 2)
    )
    value_rows = (
        jnp.concatenate([prompt_value_block, response_value_block], 0)
        .reshape(key_total_count, KEY_VALUE_HEADS, HEAD_DIM)
        .transpose(1, 0, 2)
    )
    live_rows = jnp.arange(row_count, dtype=jnp.int32) < live
    weight = jnp.where(live_rows, factor, jnp.float32(0.0))
    scaled_scores = (grads.astype(jnp.float32) * weight[:, None]).astype(jnp.bfloat16)
    query_rows = queries.reshape(row_count, KEY_VALUE_HEADS, group_index, HEAD_DIM).transpose(
        1, 2, 0, 3
    )
    group_size = scaled_scores.reshape(row_count, KEY_VALUE_HEADS, group_index, HEAD_DIM).transpose(
        1, 2, 0, 3
    )
    col = jnp.arange(key_total_count, dtype=jnp.int32)[None, :]
    row = jnp.arange(row_count, dtype=jnp.int32)[:, None]
    allowed = (col < plen) | (col - plen <= row)

    def one(parts):
        qg, gg, kg, vg = parts
        s = jnp.einsum("grd,kd->grk", qg, kg, preferred_element_type=jnp.float32) * inv
        s = jnp.where(allowed[None], s, -jnp.inf)
        top = jnp.max(s, -1, keepdims=True)
        e = jnp.exp(s - top)
        p = e / jnp.sum(e, -1, keepdims=True)
        pb = p.astype(jnp.bfloat16)
        o = jnp.einsum("grk,kd->grd", pb, vg, preferred_element_type=jnp.float32)
        delta = jnp.sum(gg.astype(jnp.float32) * o, -1, keepdims=True)
        dp = jnp.einsum("grd,kd->grk", gg, vg, preferred_element_type=jnp.float32)
        ds = (p * (dp - delta) * inv).astype(jnp.bfloat16)
        dq = jnp.einsum("grk,kd->grd", ds, kg, preferred_element_type=jnp.float32).astype(
            jnp.bfloat16
        )
        dk = jnp.einsum("grk,grd->kd", ds, qg, preferred_element_type=jnp.float32)
        dv = jnp.einsum("grk,grd->kd", pb, gg, preferred_element_type=jnp.float32)
        return (o.astype(jnp.bfloat16), dq, dk, dv)

    outs, dqs, key_gradients, value_gradients = lax.map(
        one, (query_rows, group_size, key_rows, value_rows)
    )
    attended = outs.transpose(2, 0, 1, 3).reshape(row_count, QUERY_HEADS * HEAD_DIM)
    query_grad = dqs.transpose(2, 0, 1, 3).reshape(row_count, QUERY_HEADS * HEAD_DIM)
    gradient_keys = key_gradients.transpose(1, 0, 2).reshape(
        key_total_count, KEY_VALUE_HEADS * HEAD_DIM
    )
    gradient_values = value_gradients.transpose(1, 0, 2).reshape(
        key_total_count, KEY_VALUE_HEADS * HEAD_DIM
    )
    return (
        attended,
        query_grad,
        gradient_keys[plen:].astype(jnp.bfloat16),
        gradient_values[plen:].astype(jnp.bfloat16),
        gradient_keys[:plen],
        gradient_values[:plen],
    )


def shards(
    queries,
    response_key_rows,
    response_value_rows,
    prompt_keys,
    prompt_value_rows,
    out_grad,
    resp_lengths,
):
    page_rows = prompt_keys.shape[1]
    width = prompt_keys.shape[2]
    all_keys, all_values = (
        lax.all_gather(prompt_keys, "resp", axis=1, tiled=True),
        lax.all_gather(prompt_value_rows, "resp", axis=1, tiled=True),
    )
    total = lax.psum(jnp.sum(resp_lengths.astype(jnp.float32)), ("prompt", "resp"))
    slots = lax.axis_size("prompt") * lax.axis_size("resp") * queries.shape[2]
    factor = jnp.float32(slots) / total
    att, dq, dkr, dvr, dkp, dvp = response_pass(
        queries[0, 0],
        response_key_rows[0, 0],
        response_value_rows[0, 0],
        all_keys[0],
        all_values[0],
        out_grad[0, 0],
        resp_lengths[0, 0],
        factor,
    )
    term = jnp.concatenate([dkp, dvp], 1)
    summed = lax.psum(term, "resp")
    mine = lax.dynamic_slice_in_dim(summed, lax.axis_index("resp") * page_rows, page_rows, 0)
    key_out = mine[:, :width].astype(jnp.bfloat16).reshape(1, page_rows, width)
    value_out = mine[:, width:].astype(jnp.bfloat16).reshape(1, page_rows, width)
    return (att[None, None], dq[None, None], dkr[None, None], dvr[None, None], key_out, value_out)


def solution(mesh):
    return jax.shard_map(
        shards,
        mesh=mesh,
        in_specs=(
            P("prompt", "resp", None, None),
            P("prompt", "resp", None, None),
            P("prompt", "resp", None, None),
            P("prompt", "resp", None),
            P("prompt", "resp", None),
            P("prompt", "resp", None, None),
            P("prompt", "resp"),
        ),
        out_specs=(
            P("prompt", "resp", None, None),
            P("prompt", "resp", None, None),
            P("prompt", "resp", None, None),
            P("prompt", "resp", None, None),
            P("prompt", "resp", None),
            P("prompt", "resp", None),
        ),
        check_vma=False,
    )
```

profile of v0, /device:TPU:1, one launch (start us, length us, event | category | flops | bytes accessed | tf_op | source)
XLA Modules:
  0.0 473.3 jit_solution(1671462378814914006)
XLA Ops:
  9.3 69.2 %psum.14 = f32[]{:T(128)} all-reduce(f32[]{:T(128)} %bitcast.10), channel_id=1, replica_groups=mesh['prompt'=8,'resp'=16] {'prompt','resp'}, use_global_device_ids=true, to_apply=%region_0.0 | all-reduce | flops 1 | bytes 8 | tf_op jit(solution)/shard_map/psum | solution.py:104
  78.5 4.5 copy.58
  83.4 2.4 copy.53
  86.5 2.7 fusion.52
  89.3 3.9 copy.54
  93.2 4.0 copy.56
  97.2 3.9 maximum_bitcast_fusion
  101.1 166.2 %while.17 = (s32[]{:T(128)}, bf16[8,8,128,128]{2,3,1,0:T(8,128)(2,1)}, bf16[8,8,128,128]{3,2,1,0:T(8,128)(2,1)}, f32[8,1152,128]{2,1,0:T(8,128)}, f32[8,1152,128...) while((s32[]{:T(128)}, ...), condition=%wide.region_5.6_spmd.clone, body=%wide.region_1.5_spmd.clone.sunk | while | flops 1825865856 | bytes 48037672 | solution.py:68
  101.2 5.1 %exponential_reduce_fusion.2 = (f32[8,128]{1,0:T(8,128)S(1)}, f32[8,128,1152]{2,1,0:T(8,128)}) fusion(pred[128,1152]{1,0:T(8,128)(4,1)S(1)} %fusion.89, bf16[8,1152,128]{1,2,0:T(8,128)(2,1)} %get-tuple-element.259, s32[]{:T(128)} %get-tuple-element.241, bf16[8,8,128,128]{2,3,1,0:T(8,128)(2,1)} %get-tuple-element.258), kind=kOutput, calls=%fused_computation.9.clone.1 | convolution fusion | flops 306709632 | bytes 5428224 | tf_op jit(solution)/shard_map/while/body/eval_jaxpr/sub | solution.py:54
  106.3 3.6 fusion.90
  109.9 2.6 bitcast_dynamic-update-slice_fusion.2
  112.6 2.6 fusion.91
  115.2 2.6 fusion.93
  117.8 2.4 fusion.92
  122.0 5.1 %exponential_reduce_fusion.2 = (f32[8,128]{1,0:T(8,128)S(1)}, f32[8,128,1152]{2,1,0:T(8,128)}) fusion(pred[128,1152]{1,0:T(8,128)(4,1)S(1)} %fusion.89, bf16[8,1152,128]{1,2,0:T(8,128)(2,1)} %get-tuple-element.259, s32[]{:T(128)} %get-tuple-element.241, bf16[8,8,128,128]{2,3,1,0:T(8,128)(2,1)} %get-tuple-element.258), kind=kOutput, calls=%fused_computation.9.clone.1 | convolution fusion | flops 306709632 | bytes 5428224 | tf_op jit(solution)/shard_map/while/body/eval_jaxpr/sub | solution.py:54
  127.1 3.6 fusion.90
  130.7 2.6 bitcast_dynamic-update-slice_fusion.2
  133.3 2.6 fusion.91
  135.9 2.6 fusion.93
  138.5 2.4 fusion.92
  142.8 5.1 %exponential_reduce_fusion.2 = (f32[8,128]{1,0:T(8,128)S(1)}, f32[8,128,1152]{2,1,0:T(8,128)}) fusion(pred[128,1152]{1,0:T(8,128)(4,1)S(1)} %fusion.89, bf16[8,1152,128]{1,2,0:T(8,128)(2,1)} %get-tuple-element.259, s32[]{:T(128)} %get-tuple-element.241, bf16[8,8,128,128]{2,3,1,0:T(8,128)(2,1)} %get-tuple-element.258), kind=kOutput, calls=%fused_computation.9.clone.1 | convolution fusion | flops 306709632 | bytes 5428224 | tf_op jit(solution)/shard_map/while/body/eval_jaxpr/sub | solution.py:54
  147.9 3.6 fusion.90
  151.4 2.6 bitcast_dynamic-update-slice_fusion.2
  154.1 2.6 fusion.91
  156.7 2.6 fusion.93
  159.3 2.4 fusion.92
  163.5 5.1 %exponential_reduce_fusion.2 = (f32[8,128]{1,0:T(8,128)S(1)}, f32[8,128,1152]{2,1,0:T(8,128)}) fusion(pred[128,1152]{1,0:T(8,128)(4,1)S(1)} %fusion.89, bf16[8,1152,128]{1,2,0:T(8,128)(2,1)} %get-tuple-element.259, s32[]{:T(128)} %get-tuple-element.241, bf16[8,8,128,128]{2,3,1,0:T(8,128)(2,1)} %get-tuple-element.258), kind=kOutput, calls=%fused_computation.9.clone.1 | convolution fusion | flops 306709632 | bytes 5428224 | tf_op jit(solution)/shard_map/while/body/eval_jaxpr/sub | solution.py:54
  168.7 3.6 fusion.90
  172.2 2.6 bitcast_dynamic-update-slice_fusion.2
  174.9 2.6 fusion.91
  177.5 2.6 fusion.93
  180.1 2.4 fusion.92
  184.3 5.1 %exponential_reduce_fusion.2 = (f32[8,128]{1,0:T(8,128)S(1)}, f32[8,128,1152]{2,1,0:T(8,128)}) fusion(pred[128,1152]{1,0:T(8,128)(4,1)S(1)} %fusion.89, bf16[8,1152,128]{1,2,0:T(8,128)(2,1)} %get-tuple-element.259, s32[]{:T(128)} %get-tuple-element.241, bf16[8,8,128,128]{2,3,1,0:T(8,128)(2,1)} %get-tuple-element.258), kind=kOutput, calls=%fused_computation.9.clone.1 | convolution fusion | flops 306709632 | bytes 5428224 | tf_op jit(solution)/shard_map/while/body/eval_jaxpr/sub | solution.py:54
  189.4 3.6 fusion.90
  193.0 2.6 bitcast_dynamic-update-slice_fusion.2
  195.7 2.6 fusion.91
  198.3 2.6 fusion.93
  200.9 2.4 fusion.92
  205.1 5.1 %exponential_reduce_fusion.2 = (f32[8,128]{1,0:T(8,128)S(1)}, f32[8,128,1152]{2,1,0:T(8,128)}) fusion(pred[128,1152]{1,0:T(8,128)(4,1)S(1)} %fusion.89, bf16[8,1152,128]{1,2,0:T(8,128)(2,1)} %get-tuple-element.259, s32[]{:T(128)} %get-tuple-element.241, bf16[8,8,128,128]{2,3,1,0:T(8,128)(2,1)} %get-tuple-element.258), kind=kOutput, calls=%fused_computation.9.clone.1 | convolution fusion | flops 306709632 | bytes 5428224 | tf_op jit(solution)/shard_map/while/body/eval_jaxpr/sub | solution.py:54
  210.2 3.6 fusion.90
  213.8 2.6 bitcast_dynamic-update-slice_fusion.2
  216.4 2.6 fusion.91
  219.0 2.6 fusion.93
  221.6 2.4 fusion.92
  225.8 5.1 %exponential_reduce_fusion.2 = (f32[8,128]{1,0:T(8,128)S(1)}, f32[8,128,1152]{2,1,0:T(8,128)}) fusion(pred[128,1152]{1,0:T(8,128)(4,1)S(1)} %fusion.89, bf16[8,1152,128]{1,2,0:T(8,128)(2,1)} %get-tuple-element.259, s32[]{:T(128)} %get-tuple-element.241, bf16[8,8,128,128]{2,3,1,0:T(8,128)(2,1)} %get-tuple-element.258), kind=kOutput, calls=%fused_computation.9.clone.1 | convolution fusion | flops 306709632 | bytes 5428224 | tf_op jit(solution)/shard_map/while/body/eval_jaxpr/sub | solution.py:54
  230.9 3.6 fusion.90
  234.5 2.6 bitcast_dynamic-update-slice_fusion.2
  237.1 2.6 fusion.91
  239.8 2.6 fusion.93
  242.4 2.4 fusion.92
  244.8 1.7 fusion.94
  246.6 5.1 %exponential_reduce_fusion.2 = (f32[8,128]{1,0:T(8,128)S(1)}, f32[8,128,1152]{2,1,0:T(8,128)}) fusion(pred[128,1152]{1,0:T(8,128)(4,1)S(1)} %fusion.89, bf16[8,1152,128]{1,2,0:T(8,128)(2,1)} %get-tuple-element.259, s32[]{:T(128)} %get-tuple-element.241, bf16[8,8,128,128]{2,3,1,0:T(8,128)(2,1)} %get-tuple-element.258), kind=kOutput, calls=%fused_computation.9.clone.1 | convolution fusion | flops 306709632 | bytes 5428224 | tf_op jit(solution)/shard_map/while/body/eval_jaxpr/sub | solution.py:54
  251.7 3.6 fusion.90
  255.3 2.6 bitcast_dynamic-update-slice_fusion.2
  257.9 2.6 fusion.91
  260.5 2.6 fusion.93
  263.1 2.4 fusion.92
  265.6 1.7 fusion.94
  267.3 2.9 copy_bitcast_fusion.1
  272.0 3.8 pad_maximum_fusion
  275.8 177.7 %all-reduce.1 = bf16[1024,2048]{1,0:T(8,128)(2,1)} all-reduce(f32[1024,2048]{1,0:T(8,128)} %pad_maximum_fusion), channel_id=1, replica_groups=mesh['prompt'=8,'resp'=16] {'resp'}, use_global_device_ids=true, to_apply=%region_6.7 | all-reduce | flops 2097152 | bytes 12582912 | tf_op jit(solution)/shard_map/psum | solution.py:118
  457.1 2.9 copy.63
  460.1 2.3 broadcast_in_dim_reshape.7
  462.4 4.1 copy.73
  (97 shorter events, 18.6 us)
Async XLA Ops:
  7.2 82.1 %all-gather.3.cloned.1.call-start = ((), (), s32[]{:S(2)}) async-start(), calls=%async_computation | async-start | bytes 2228224 | tf_op jit(solution)/shard_map/all_gather | solution.py:101
  7.9 85.3 %all-gather.5.cloned.1.call-start = ((), (), s32[]{:S(2)}) async-start(), calls=%async_computation.1 | async-start | bytes 2228224 | tf_op jit(solution)/shard_map/all_gather | solution.py:102
  78.5 4.5 copy-start.1
  78.5 4.7 copy-start.2
  78.5 4.9 %copy-start = (bf16[1,1,128,8192]{3,2,1,0:T(8,128)(2,1)S(1)}, bf16[1,1,128,8192]{3,2,1,0:T(8,128)(2,1)}, u32[]{:S(2)}) copy-start(bf16[1,1,128,8192]{3,2,1,0:T(8,128)(2,1)} %param.9) | copy-start | bytes 6291460
  106.3 6.2 %slice-start = ((s8[4718592]{0:T(1024)(128)(4,1)}), s8[4194304]{0:T(1024)(128)(4,1)S(1)}, s32[]{:S(2)}) async-start(s8[4718592]{0:T(1024)(128)(4,1)} %bitcast.136), calls=%async_computation.2 | async-start | bytes 8388608 | tf_op jit(solution)/shard_map/while
  106.3 6.2 %slice-start.1 = ((s8[4718592]{0:T(1024)(128)(4,1)}), s8[524288]{0:T(1024)(128)(4,1)S(1)}, s32[]{:S(2)}) async-start(s8[4718592]{0:T(1024)(128)(4,1)} %bitcast.136), calls=%async_computation.3 | async-start | bytes 1048576 | tf_op jit(solution)/shard_map/while
  127.1 6.2 %slice-start = ((s8[4718592]{0:T(1024)(128)(4,1)}), s8[4194304]{0:T(1024)(128)(4,1)S(1)}, s32[]{:S(2)}) async-start(s8[4718592]{0:T(1024)(128)(4,1)} %bitcast.136), calls=%async_computation.2 | async-start | bytes 8388608 | tf_op jit(solution)/shard_map/while
  127.1 6.2 %slice-start.1 = ((s8[4718592]{0:T(1024)(128)(4,1)}), s8[524288]{0:T(1024)(128)(4,1)S(1)}, s32[]{:S(2)}) async-start(s8[4718592]{0:T(1024)(128)(4,1)} %bitcast.136), calls=%async_computation.3 | async-start | bytes 1048576 | tf_op jit(solution)/shard_map/while
  147.9 6.2 %slice-start = ((s8[4718592]{0:T(1024)(128)(4,1)}), s8[4194304]{0:T(1024)(128)(4,1)S(1)}, s32[]{:S(2)}) async-start(s8[4718592]{0:T(1024)(128)(4,1)} %bitcast.136), calls=%async_computation.2 | async-start | bytes 8388608 | tf_op jit(solution)/shard_map/while
  147.9 6.2 %slice-start.1 = ((s8[4718592]{0:T(1024)(128)(4,1)}), s8[524288]{0:T(1024)(128)(4,1)S(1)}, s32[]{:S(2)}) async-start(s8[4718592]{0:T(1024)(128)(4,1)} %bitcast.136), calls=%async_computation.3 | async-start | bytes 1048576 | tf_op jit(solution)/shard_map/while
  168.7 6.2 %slice-start = ((s8[4718592]{0:T(1024)(128)(4,1)}), s8[4194304]{0:T(1024)(128)(4,1)S(1)}, s32[]{:S(2)}) async-start(s8[4718592]{0:T(1024)(128)(4,1)} %bitcast.136), calls=%async_computation.2 | async-start | bytes 8388608 | tf_op jit(solution)/shard_map/while
  168.7 6.2 %slice-start.1 = ((s8[4718592]{0:T(1024)(128)(4,1)}), s8[524288]{0:T(1024)(128)(4,1)S(1)}, s32[]{:S(2)}) async-start(s8[4718592]{0:T(1024)(128)(4,1)} %bitcast.136), calls=%async_computation.3 | async-start | bytes 1048576 | tf_op jit(solution)/shard_map/while
  189.4 6.2 %slice-start = ((s8[4718592]{0:T(1024)(128)(4,1)}), s8[4194304]{0:T(1024)(128)(4,1)S(1)}, s32[]{:S(2)}) async-start(s8[4718592]{0:T(1024)(128)(4,1)} %bitcast.136), calls=%async_computation.2 | async-start | bytes 8388608 | tf_op jit(solution)/shard_map/while
  189.4 6.2 %slice-start.1 = ((s8[4718592]{0:T(1024)(128)(4,1)}), s8[524288]{0:T(1024)(128)(4,1)S(1)}, s32[]{:S(2)}) async-start(s8[4718592]{0:T(1024)(128)(4,1)} %bitcast.136), calls=%async_computation.3 | async-start | bytes 1048576 | tf_op jit(solution)/shard_map/while
  210.2 6.2 %slice-start = ((s8[4718592]{0:T(1024)(128)(4,1)}), s8[4194304]{0:T(1024)(128)(4,1)S(1)}, s32[]{:S(2)}) async-start(s8[4718592]{0:T(1024)(128)(4,1)} %bitcast.136), calls=%async_computation.2 | async-start | bytes 8388608 | tf_op jit(solution)/shard_map/while
  210.2 6.2 %slice-start.1 = ((s8[4718592]{0:T(1024)(128)(4,1)}), s8[524288]{0:T(1024)(128)(4,1)S(1)}, s32[]{:S(2)}) async-start(s8[4718592]{0:T(1024)(128)(4,1)} %bitcast.136), calls=%async_computation.3 | async-start | bytes 1048576 | tf_op jit(solution)/shard_map/while
  230.9 6.2 %slice-start = ((s8[4718592]{0:T(1024)(128)(4,1)}), s8[4194304]{0:T(1024)(128)(4,1)S(1)}, s32[]{:S(2)}) async-start(s8[4718592]{0:T(1024)(128)(4,1)} %bitcast.136), calls=%async_computation.2 | async-start | bytes 8388608 | tf_op jit(solution)/shard_map/while
  230.9 6.2 %slice-start.1 = ((s8[4718592]{0:T(1024)(128)(4,1)}), s8[524288]{0:T(1024)(128)(4,1)S(1)}, s32[]{:S(2)}) async-start(s8[4718592]{0:T(1024)(128)(4,1)} %bitcast.136), calls=%async_computation.3 | async-start | bytes 1048576 | tf_op jit(solution)/shard_map/while
  251.7 6.2 %slice-start = ((s8[4718592]{0:T(1024)(128)(4,1)}), s8[4194304]{0:T(1024)(128)(4,1)S(1)}, s32[]{:S(2)}) async-start(s8[4718592]{0:T(1024)(128)(4,1)} %bitcast.136), calls=%async_computation.2 | async-start | bytes 8388608 | tf_op jit(solution)/shard_map/while
  251.7 6.2 %slice-start.1 = ((s8[4718592]{0:T(1024)(128)(4,1)}), s8[524288]{0:T(1024)(128)(4,1)S(1)}, s32[]{:S(2)}) async-start(s8[4718592]{0:T(1024)(128)(4,1)} %bitcast.136), calls=%async_computation.3 | async-start | bytes 1048576 | tf_op jit(solution)/shard_map/while
  267.3 4.0 slice-start.2
  267.3 4.0 slice-start.3
Sparse Core Ops, SparseCore 0:
  9.7 37.8 all-gather.2
  49.3 34.1 all-gather.4
where the time goes:
time: 475 us; the launch traced here: 473 us
  blocking collectives  247 us (52%)
  matrix products  136 us (29%)
  other arithmetic  40.2 us (8%)
  local copies, waits for them, and re-layouts  32.9 us (7%)
  between operations  15.5 us (3%)
    psum x1, blocking collectives, shards(): summed = lax.psum(term, 'resp')  178 us
    psum x1, blocking collectives, shards(): lax.psum(jnp.sum(resp_lengths.astype(jnp.float32)), ('prompt', 'resp'))  69.2 us
    sub x8, matrix products, one(): e = jnp.exp(s - top)  40.9 us
    convert_element_type x8, other arithmetic, one(): pb = p.astype(jnp.bfloat16)  28.4 us
    dot_general x8, matrix products, one(): dp = jnp.einsum('grd,kd->grk', gg, vg, preferred_element_type=jnp.float32)  20.9 us
    dot_general x8, matrix products, one(): dk = jnp.einsum('grk,grd->kd', ds, qg, preferred_element_type=jnp.float32)  20.8 us
    dot_general x8, matrix products, one(): o = jnp.einsum('grk,kd->grd', pb, vg, preferred_element_type=jnp.float32)  20.6 us
    dot_general x8, matrix products, one(): jnp.einsum('grk,kd->grd', ds, kg, preferred_element_type=jnp.float32)  19.6 us
  transfers between devices with their start and end apart: 2, of which 0 were waited for; matrix products, arithmetic and copies ran while one was open for 3% of the time, Pallas kernels for 0%

commit v1 on v0

v1 whole, which is shorter than its diff:
```python
import jax
import jax.numpy as jnp
from jax import lax
from jax.experimental import pallas as pl
from jax.experimental.pallas import tpu as pltpu
from jax.sharding import PartitionSpec as P

F32, BF16 = jnp.float32, jnp.bfloat16
QUERY_HEADS = 64
KEY_VALUE_HEADS = 8
GROUP = QUERY_HEADS // KEY_VALUE_HEADS
D = 128
INV = 1.0 / D**0.5
LOG2E = 1.4426950408889634


def dot(a, b, ca, cb):
    return lax.dot_general(a, b, (((ca,), (cb,)), ((), ())), preferred_element_type=F32)


def attention_kernel(
    weight_ref, live_ref, q_ref, g_ref, kp_ref, vp_ref, kr_ref, vr_ref,
    att_ref, dq_ref, dkr_ref, dvr_ref, dkv_ref,
):
    tokens = q_ref.shape[0]
    heads = 4
    rows = heads * tokens
    plen = kp_ref.shape[0]
    factor = weight_ref[0, 0]
    live = live_ref[0, 0]
    token = lax.broadcasted_iota(jnp.int32, (rows, 128), 0) % tokens
    key = lax.broadcasted_iota(jnp.int32, (rows, 128), 1)
    seen = key <= token
    weight = jnp.where(token[:, :1] < live, factor, 0.0)

    def head(h, _):
        cols = pl.ds(pl.multiple_of(h * D, D), D)
        keys = jnp.concatenate([kp_ref[:, cols], kr_ref[:, cols]], 0)
        values = jnp.concatenate([vp_ref[:, cols], vr_ref[:, cols]], 0)

        def columns(j):
            return [
                pl.ds(pl.multiple_of((h * GROUP + j * heads + i) * D, D), D)
                for i in range(heads)
            ]

        def first(j):
            q = jnp.concatenate([q_ref[:, c] for c in columns(j)], 0)
            g = jnp.concatenate([g_ref[:, c] for c in columns(j)], 0)
            g = (g.astype(F32) * weight).astype(BF16)
            return q, g, dot(q, keys, 1, 1), dot(g, values, 1, 1)

        totals = [None, None]

        def rest(j, state):
            q, g, s, dp = state
            s = jnp.concatenate([s[:, :plen], jnp.where(seen, s[:, plen:], -1e30)], 1)
            top = jnp.max(s, 1, keepdims=True)
            e = jnp.exp2(s * (INV * LOG2E) - top * (INV * LOG2E))
            scale = 1.0 / jnp.sum(e, 1, keepdims=True)
            e = e.astype(BF16)
            o = dot(e, values, 1, 0) * scale
            gf = g.astype(F32)
            delta = jnp.sum(gf * o, 1, keepdims=True)
            ds = e * (dp - delta).astype(BF16)
            dq = dot(ds, keys, 1, 0) * (scale * INV)
            for i, c in enumerate(columns(j)):
                att_ref[:, c] = o[i * tokens : (i + 1) * tokens].astype(BF16)
                dq_ref[:, c] = dq[i * tokens : (i + 1) * tokens].astype(BF16)
            g = (gf * scale).astype(BF16)
            q = (q.astype(F32) * scale).astype(BF16)
            dk, dv = dot(q.T, ds, 1, 0), dot(g.T, e, 1, 0)
            totals[0] = dk if totals[0] is None else totals[0] + dk
            totals[1] = dv if totals[1] is None else totals[1] + dv

        state = first(0)
        for j in range(GROUP // heads):
            after = first(j + 1) if j + 1 < GROUP // heads else None
            rest(j, state)
            state = after
        dk = (totals[0].T * INV).astype(BF16)
        dv = totals[1].T.astype(BF16)
        dkr_ref[:, cols] = dk[plen:]
        dvr_ref[:, cols] = dv[plen:]
        dkv_ref[h, 0] = dk[:plen]
        dkv_ref[h, 1] = dv[:plen]
        return 0

    lax.fori_loop(0, KEY_VALUE_HEADS, head, 0)


def attention(weight, live, q, g, kp, vp, kr, vr):
    vmem = pl.BlockSpec(memory_space=pltpu.VMEM)
    smem = pl.BlockSpec(memory_space=pltpu.SMEM)
    return pl.pallas_call(
        attention_kernel,
        out_shape=(
            jax.ShapeDtypeStruct(q.shape, BF16),
            jax.ShapeDtypeStruct(q.shape, BF16),
            jax.ShapeDtypeStruct(kr.shape, BF16),
            jax.ShapeDtypeStruct(kr.shape, BF16),
            jax.ShapeDtypeStruct((KEY_VALUE_HEADS, 2, kp.shape[0], D), BF16),
        ),
        in_specs=[smem, smem] + [vmem] * 6,
        out_specs=(vmem,) * 5,
        compiler_params=pltpu.CompilerParams(vmem_limit_bytes=56 * 2**20),
        name="attention",
    )(weight, live, q, g, kp, vp, kr, vr)


def shards(q, kr, vr, kp, vp, g, lengths):
    rows, width = kp.shape[1:]
    kv = lax.all_gather(jnp.concatenate([kp, vp], 2), "resp", axis=1, tiled=True)[0]
    total = lax.psum(jnp.sum(lengths.astype(F32)), ("prompt", "resp"))
    slots = lax.axis_size("prompt") * lax.axis_size("resp") * q.shape[2]
    factor = jnp.full((1, 1), slots, F32) / total
    att, dq, dkr, dvr, dkv = attention(
        factor, lengths, q[0, 0], g[0, 0], kv[:, :width], kv[:, width:], kr[0, 0], vr[0, 0]
    )
    mine = lax.psum_scatter(dkv, "resp", scatter_dimension=2, tiled=True)
    mine = mine.transpose(1, 2, 0, 3).reshape(2, rows, width)
    return att[None, None], dq[None, None], dkr[None, None], dvr[None, None], mine[:1], mine[1:]


def solution(mesh):
    four = P("prompt", "resp", None, None)
    three = P("prompt", "resp", None)
    return jax.shard_map(
        shards,
        mesh=mesh,
        in_specs=(four, four, four, three, three, four, P("prompt", "resp")),
        out_specs=(four, four, four, four, three, three),
        check_vma=False,
    )
```

time: 475 us -> 203 us (0.43)
  blocking collectives: 247 us -> 69.2 us
  matrix products: 136 us -> 0 us
  waiting for transfers between devices: 1.4 us -> 64.1 us
  Pallas kernels: 0 us -> 43.7 us
  other arithmetic: 40.2 us -> 1.69 us
  local copies, waits for them, and re-layouts: 32.9 us -> 6.35 us
    psum x2 -> x1, blocking collectives: 247 us -> 69.2 us  [shards(): total = lax.psum(jnp.sum(lengths.astype(F32)), ('prompt', 'resp'))]
    dot_general x40 -> x0, matrix products: 95.1 us -> none  [the longest x8 20.9 us: one(): dp = jnp.einsum('grd,kd->grk', gg, vg, preferred_element_type=jnp.float32)]
    reduce_scatter x0 -> x1, waiting for transfers between devices: none -> 64 us  [shards(): mine = lax.psum_scatter(dkv, 'resp', scatter_dimension=2, tiled=True)]
    pallas_call x0 -> x1, Pallas kernels: none -> 43.7 us  [attention(): pl.pallas_call(attention_kernel, out_shape=(jax.ShapeDtypeStruct(q.shape,...]
    sub x8 -> x0, matrix products: 40.9 us -> none  [one(): e = jnp.exp(s - top)]
    convert_element_type x8 -> x0, other arithmetic: 28.4 us -> none  [one(): pb = p.astype(jnp.bfloat16)]
    all_gather x2 -> x0, local copies, waits for them, and re-layouts: 7.91 us -> none  [the longest x1 3.96 us: shards(): lax.all_gather(prompt_value_rows, 'resp', axis=1, tiled=True)]
    another operation x3 -> x0, local copies, waits for them, and re-layouts: 7.33 us -> none  [the longest x1 4.06 us: shards(): att[None, None]]
  transfers between devices with their start and end apart: 2 -> 2, of which waited for: 0 -> 1; matrix products, arithmetic and copies ran while one was open for 3% -> 0% of each run, Pallas kernels for 0% -> 0%
where the time goes in v1:
time: 203 us; the launch traced here: 200 us
  blocking collectives  69.2 us (34%)
  waiting for transfers between devices  64.1 us (32%)
  Pallas kernels  43.7 us (22%)
  between operations  15.4 us (8%)
  local copies, waits for them, and re-layouts  6.35 us (3%)
    psum x1, blocking collectives, shards(): total = lax.psum(jnp.sum(lengths.astype(F32)), ('prompt', 'resp'))  69.2 us
    reduce_scatter x1, waiting for transfers between devices, shards(): mine = lax.psum_scatter(dkv, 'resp', scatter_dimension=2, tiled=True)  64 us
    pallas_call x1, Pallas kernels, attention(): pl.pallas_call(attention_kernel, out_shape=(jax.ShapeDtypeStruct(q.shape,...  43.7 us
    slice x1, local copies, waits for them, and re-layouts, shards(): kv[:, width:]  4.63 us
  transfers between devices with their start and end apart: 2, of which 1 were waited for; matrix products, arithmetic and copies ran while one was open for 0% of the time, Pallas kernels for 0%

profile of v1, /device:TPU:1, one launch (start us, length us, event | category | flops | bytes accessed | tf_op | source)
XLA Modules:
  0.0 200.5 jit_solution(4814657204000685106)
XLA Ops:
  7.2 0.0 all-gather.2.cloned.1.call-start
  7.2 1.7 pad_maximum_fusion
  8.9 0.0 all-gather.2.cloned.1.call-update
  8.9 0.0 reduce-scatter.2.cloned.1.call-start
  9.6 69.2 %psum.7 = f32[]{:T(128)} all-reduce(f32[]{:T(128)} %bitcast), channel_id=1, replica_groups=mesh['prompt'=8,'resp'=16] {'prompt','resp'}, use_global_device_ids=true, to_apply=%region_0.0 | all-reduce | flops 1 | bytes 8 | tf_op jit(solution)/shard_map/psum | solution.py:114
  79.5 0.0 all-gather.2.cloned.1.call-done
  79.5 4.6 %fusion = (bf16[1024,1024]{1,0:T(8,128)(2,1)}, bf16[1024,1024]{1,0:T(8,128)(2,1)}) fusion(bf16[1024,2048]{1,0:T(8,128)(2,1)} %bitcast.20), kind=kLoop, calls=%fused_computation.5 | loop fusion | bytes 8388608 | tf_op jit(solution)/shard_map/slice | solution.py:118
  84.2 43.7 %attention.1 = (bf16[128,8192]{1,0:T(8,128)(2,1)}, bf16[128,8192]{1,0:T(8,128)(2,1)}, bf16[128,1024]{1,0:T(8,128)(2,1)}, bf16[128,1024]{1,0:T(8,128)(2,1)}, bf16[8,2,1024,128]{3,2,1,0:T(8,128)(2,1)}) custom-call(f32[1,1]{1,0:T(1,128)} %bitcast.1.weight_ref, s32[1,1]{1,0:T(1,128)S(6)} %copy.19.live_ref, bf16[128,8192]{1,0:T(8,128)(2,1)} %bitcast.21, ...), custom_call_target="tpu_custom_call" | custom-call | tf_op jit(solution)/shard_map/attention/pallas_call | solution.py:95
  127.9 0.0 reduce-scatter.2.cloned.1.call-update
  127.9 64.0 %reduce-scatter.2.cloned.1.call-done = bf16[8,2,64,128]{3,2,1,0:T(8,128)(2,1)} async-done(((bf16[8,2,1024,128]{3,2,1,0:T(8,128)(2,1)}), bf16[8,2,64,128]{3,2,1,0:T(8,128)(2,1)}) %reduce-scatter.2.cloned.1.call-update) | async-done | bytes 262160 | tf_op jit(solution)/shard_map/reduce_scatter | solution.py:120
  191.9 1.0 slice_bitcast_fusion
  192.9 0.7 copy_bitcast_fusion
Async XLA Ops:
  7.2 72.4 %all-gather.2.cloned.1.call-start = ((), (), s32[]{:S(2)}) async-start(), calls=%async_computation.1 | async-start | bytes 4456448 | tf_op jit(solution)/shard_map/all_gather | solution.py:113
  8.9 183.0 %reduce-scatter.2.cloned.1.call-start = ((), (), s32[]{:S(2)}) async-start(), calls=%async_computation.2 | async-start | bytes 4456448 | tf_op jit(solution)/shard_map/reduce_scatter | solution.py:120
Sparse Core Ops, SparseCore 0:
  10.3 41.3 all-gather.1
  128.0 63.8 reduce-scatter.1

commit v2 on v1

v2 whole, which is shorter than its diff:
```python
import functools

import jax
import jax.numpy as jnp
from jax import lax
from jax.experimental import pallas as pl
from jax.experimental.pallas import tpu as pltpu
from jax.sharding import PartitionSpec as P

F32, BF16 = jnp.float32, jnp.bfloat16
QUERY_HEADS = 64
KEY_VALUE_HEADS = 8
GROUP = QUERY_HEADS // KEY_VALUE_HEADS
D = 128
INV = 1.0 / D**0.5
LOG2E = 1.4426950408889634
BLOCK_HEADS = 4
Z, Y, CORES = 4, 2, 2
MESH = pl.DeviceIdType.MESH


def dot(a, b, ca, cb):
    return lax.dot_general(a, b, (((ca,), (cb,)), ((), ())), preferred_element_type=F32)


def kernel(
    prompts, live_ref, q_hbm, g_hbm, kp_hbm, vp_hbm, kr_hbm, vr_hbm,
    att_hbm, dq_hbm, dkr_ref, dvr_ref, pk_ref, pv_ref,
    kv, q_ref, g_ref, att_ref, dq_ref, grad,
    pair_out, pair_in, far_out, far_in, near_out, near_in, last_out, last_in,
    lens_out, lens_in, factor_ref,
    load_sem, store_sem, ag_send, ag_recv, rs_send, rs_recv, len_send, len_recv,
):
    heads = KEY_VALUE_HEADS
    tokens = q_ref.shape[0]
    page = kp_hbm.shape[0]
    strip = Y * page
    plane = Z * strip
    plen = CORES * plane
    me = lax.axis_index("resp")
    prompt = lax.axis_index("prompt")
    z, y, c = me // (Y * CORES), (me // CORES) % Y, me % CORES
    up, down, over = (z + 1) % Z, (z + Z - 1) % Z, (z + 2) % Z

    def at(zz, yy, cc):
        return {"resp": (zz * Y + yy) * CORES + cc}

    sibling, beside = at(z, y, 1 - c), at(z, 1 - y, c)
    above, below = at(up, y, c), at(down, y, c)
    corner = at(z, 1 - y, 1 - c)
    len_peers = [
        [sibling, beside, corner],
        [above, below, at(over, y, c)],
        [{"prompt": (prompt + k) % prompts} for k in range(1, prompts)],
    ]

    def page_rows(cc, zz, yy):
        return pl.ds(pl.multiple_of(cc * plane + zz * strip + yy * page, page), page)

    def strip_rows(cc, zz):
        return pl.ds(pl.multiple_of(cc * plane + zz * strip, strip), strip)

    def plane_rows(cc):
        return pl.ds(pl.multiple_of(cc * plane, plane), plane)

    def columns(h):
        return pl.ds(pl.multiple_of(h * D, D), D)

    def block(h):
        return pl.ds(pl.multiple_of(h * GROUP * D, GROUP * D), GROUP * D)

    def load(h, i):
        mine, extra = page_rows(c, z, y), pl.ds(plen, tokens)
        src, dst = [
            lambda: (kp_hbm.at[:, columns(h)], kv.at[h, 0, mine, :]),
            lambda: (vp_hbm.at[:, columns(h)], kv.at[h, 1, mine, :]),
            lambda: (kr_hbm.at[:, columns(h)], kv.at[h, 0, extra, :]),
            lambda: (vr_hbm.at[:, columns(h)], kv.at[h, 1, extra, :]),
            lambda: (q_hbm.at[:, block(h)], q_ref.at[:, block(h)]),
            lambda: (g_hbm.at[:, block(h)], g_ref.at[:, block(h)]),
        ][i]()
        return pltpu.make_async_copy(src, dst, load_sem.at[h, i])

    def stores(h):
        return [
            pltpu.make_async_copy(a.at[:, block(h)], b.at[:, block(h)], store_sem.at[h, i])
            for i, (a, b) in enumerate([(att_ref, att_hbm), (dq_ref, dq_hbm)])
        ]

    def gather_copy(h, k, rows, to):
        return pltpu.make_async_remote_copy(
            kv.at[h, :, rows, :], kv.at[h, :, rows, :],
            ag_send.at[h, k], ag_recv.at[h, k], device_id=to, device_id_type=MESH,
        )

    def gather1(h):
        mine = page_rows(c, z, y)
        for i in range(2):
            load(h, i).wait()
        gather_copy(h, 0, mine, beside).start()
        gather_copy(h, 1, mine, above).start()
        gather_copy(h, 2, mine, below).start()
        gather_copy(h, 3, mine, sibling).start()

    def gather2(h):
        other = page_rows(c, z, 1 - y)
        gather_copy(h, 0, other, beside).wait_recv()
        gather_copy(h, 4, other, above).start()
        gather_copy(h, 5, other, below).start()
        gather_copy(h, 6, other, sibling).start()

    def gather3(h):
        gather_copy(h, 1, page_rows(c, down, y), below).wait_recv()
        gather_copy(h, 4, page_rows(c, down, 1 - y), below).wait_recv()
        gather_copy(h, 7, page_rows(c, down, 0), above).start()
        gather_copy(h, 2, page_rows(c, up, y), above).wait_recv()
        gather_copy(h, 5, page_rows(c, up, 1 - y), above).wait_recv()
        gather_copy(h, 8, page_rows(c, up, 1), below).start()
        gather_copy(h, 9, strip_rows(c, down), sibling).start()
        gather_copy(h, 10, strip_rows(c, up), sibling).start()

    def gather4(h):
        gather_copy(h, 7, page_rows(c, over, 0), below).wait_recv()
        gather_copy(h, 8, page_rows(c, over, 1), above).wait_recv()
        gather_copy(h, 11, strip_rows(c, over), sibling).start()

    def gathered(h):
        d = 1 - c
        gather_copy(h, 3, page_rows(d, z, y), sibling).wait_recv()
        gather_copy(h, 6, page_rows(d, z, 1 - y), sibling).wait_recv()
        gather_copy(h, 9, strip_rows(d, down), sibling).wait_recv()
        gather_copy(h, 10, strip_rows(d, up), sibling).wait_recv()
        gather_copy(h, 11, strip_rows(d, over), sibling).wait_recv()
        for i in range(2, 6):
            load(h, i).wait()

    def sum_ends(h, k):
        return [
            lambda: (pair_out.at[h], pair_in.at[h], sibling),
            lambda: (far_out.at[h, 0], far_in.at[h, 0], above),
            lambda: (far_out.at[h, 1], far_in.at[h, 1], below),
            lambda: (near_out.at[h, 0], near_in.at[h, 0], above),
            lambda: (near_out.at[h, 1], near_in.at[h, 1], below),
            lambda: (last_out.at[h], last_in.at[h], beside),
        ][k]()

    def sum_copy(h, k):
        src, dst, to = sum_ends(h, k)
        return pltpu.make_async_remote_copy(
            src, dst, rs_send.at[h, k], rs_recv.at[h, k], device_id=to, device_id_type=MESH
        )

    def sum0(h):
        pair_out[h] = grad[h % 4, :, plane_rows(1 - c), :].astype(BF16)
        sum_copy(h, 0).start()

    def sum1(h):
        sum_copy(h, 0).wait_recv()
        rows = plane_rows(c)
        grad[h % 4, :, rows, :] += pair_in[h].astype(F32)
        far_out[h, 0] = grad[h % 4, :, page_rows(c, over, 0), :].astype(BF16)
        sum_copy(h, 1).start()
        far_out[h, 1] = grad[h % 4, :, page_rows(c, over, 1), :].astype(BF16)
        sum_copy(h, 2).start()

    def sum2(h):
        sum_copy(h, 1).wait_recv()
        grad[h % 4, :, page_rows(c, up, 0), :] += far_in[h, 0].astype(F32)
        near_out[h, 0] = grad[h % 4, :, strip_rows(c, up), :].astype(BF16)
        sum_copy(h, 3).start()
        sum_copy(h, 2).wait_recv()
        grad[h % 4, :, page_rows(c, down, 1), :] += far_in[h, 1].astype(F32)
        near_out[h, 1] = grad[h % 4, :, strip_rows(c, down), :].astype(BF16)
        sum_copy(h, 4).start()

    def sum3(h):
        sum_copy(h, 3).wait_recv()
        sum_copy(h, 4).wait_recv()
        grad[h % 4, :, strip_rows(c, z), :] += near_in[h, 0].astype(F32) + near_in[h, 1].astype(F32)
        last_out[h] = grad[h % 4, :, page_rows(c, z, 1 - y), :].astype(BF16)
        sum_copy(h, 5).start()

    def sum4(h):
        sum_copy(h, 5).wait_recv()
        total = grad[h % 4, :, page_rows(c, z, y), :] + last_in[h].astype(F32)
        factor = factor_ref[0:1, :]
        pk_ref[:, columns(h)] = (total[0] * (factor * INV)).astype(BF16)
        pv_ref[:, columns(h)] = (total[1] * factor).astype(BF16)

    def len_slot(stage, i):
        return sum(len(p) for p in len_peers[:stage]) + i

    def len_copies(stage):
        return [
            pltpu.make_async_remote_copy(
                lens_out.at[stage], lens_in.at[len_slot(stage, i)],
                len_send.at[len_slot(stage, i)], len_recv.at[len_slot(stage, i)],
                device_id=peer, device_id_type=MESH,
            )
            for i, peer in enumerate(len_peers[stage])
        ]

    def len_start(stage):
        for copy in len_copies(stage):
            copy.start()

    def len_sum(stage):
        total = lens_out[stage]
        for i, copy in enumerate(len_copies(stage)):
            copy.wait_recv()
            total = total + lens_in[len_slot(stage, i)]
        return total

    rows = BLOCK_HEADS * tokens
    live = live_ref[0, 0]

    def first(h, j, keys, values):
        cols = [columns(h * GROUP + j * BLOCK_HEADS + i) for i in range(BLOCK_HEADS)]
        token = lax.broadcasted_iota(jnp.int32, (rows, 1), 0) % tokens
        q = jnp.concatenate([q_ref[:, k] for k in cols], 0)
        g = jnp.concatenate([g_ref[:, k] for k in cols], 0)
        g = jnp.where(token < live, g.astype(F32), 0.0).astype(BF16)
        return q, g, dot(q, keys, 1, 1), dot(g, values, 1, 1)

    def rest(h, j, keys, values, state, totals):
        q, g, s, dp = state
        cols = [columns(h * GROUP + j * BLOCK_HEADS + i) for i in range(BLOCK_HEADS)]
        token = lax.broadcasted_iota(jnp.int32, (rows, tokens), 0) % tokens
        key = lax.broadcasted_iota(jnp.int32, (rows, tokens), 1)
        s = jnp.concatenate([s[:, :plen], jnp.where(key <= token, s[:, plen:], -1e30)], 1)
        top = jnp.max(s, 1, keepdims=True)
        e = jnp.exp2(s * (INV * LOG2E) - top * (INV * LOG2E))
        scale = 1.0 / jnp.sum(e, 1, keepdims=True)
        e = e.astype(BF16)
        o = dot(e, values, 1, 0) * scale
        gf = g.astype(F32)
        delta = jnp.sum(gf * o, 1, keepdims=True)
        ds = e * (dp - delta).astype(BF16)
        dq = dot(ds, keys, 1, 0) * (scale * INV) * factor_ref[0:1, :]
        for i, k in enumerate(cols):
            att_ref[:, k] = o[i * tokens : (i + 1) * tokens].astype(BF16)
            dq_ref[:, k] = dq[i * tokens : (i + 1) * tokens].astype(BF16)
        g = (gf * scale).astype(BF16)
        q = (q.astype(F32) * scale).astype(BF16)
        dk, dv = dot(q.T, ds, 1, 0), dot(g.T, e, 1, 0)
        return (dk, dv) if totals is None else (totals[0] + dk, totals[1] + dv)

    def when(condition, stage, h):
        pl.when(condition)(functools.partial(stage, h))

    def head(h, _):
        when(h + 2 < heads, gather2, h + 2)
        when(h >= 2, sum2, h - 2)
        when(h >= 3, sum4, h - 3)
        gathered(h)
        keys, values = kv[h, 0], kv[h, 1]
        blocks = GROUP // BLOCK_HEADS
        state, totals = first(h, 0, keys, values), None
        for j in range(blocks):
            after = first(h, j + 1, keys, values) if j + 1 < blocks else None
            totals = rest(h, j, keys, values, state, totals)
            state = after
            if j == 0:
                when(h + 3 < heads, gather1, h + 3)
                when(h + 1 < heads, gather4, h + 1)
                when(h + 2 < heads, gather3, h + 2)
                when(h >= 1, sum1, h - 1)
                when(h >= 2, sum3, h - 2)
        dk, dv = totals[0].T, totals[1].T
        grad[h % 4, 0] = dk
        grad[h % 4, 1] = dv
        sum0(h)
        for copy in stores(h):
            copy.start()
        factor = factor_ref[0:1, :]
        dkr_ref[:, columns(h)] = (dk[plen:] * (factor * INV)).astype(BF16)
        dvr_ref[:, columns(h)] = (dv[plen:] * factor).astype(BF16)
        return 0

    def start_loads(h, _):
        for i in range(6):
            load(h, i).start()
        return 0

    lax.fori_loop(0, heads, start_loads, 0)
    lens_out[0] = jnp.full(lens_out.shape[1:], live.astype(F32))
    barrier = pltpu.get_barrier_semaphore()
    peers = [p for stage in len_peers for p in stage]
    for p in peers:
        pl.semaphore_signal(barrier, inc=1, device_id=p, device_id_type=MESH)
    pl.semaphore_wait(barrier, len(peers))

    gather1(0)
    len_start(0)
    gather1(1)
    gather2(0)
    lens_out[1] = len_sum(0)
    len_start(1)
    gather2(1)
    gather3(0)
    lens_out[2] = len_sum(1)
    len_start(2)
    gather1(2)
    gather4(0)
    gather3(1)
    factor_ref[...] = (prompts * Z * Y * CORES * tokens) / len_sum(2)

    lax.fori_loop(0, heads, head, 0)

    n = heads
    sum2(n - 2)
    sum4(n - 3)
    sum1(n - 1)
    sum3(n - 2)
    sum2(n - 1)
    sum4(n - 2)
    sum3(n - 1)
    sum4(n - 1)

    def finish(h, _):
        for k in range(12):
            rows_k = strip_rows(c, z) if k >= 9 else page_rows(c, z, y)
            gather_copy(h, k, rows_k, sibling).wait_send()
        for k in range(6):
            sum_copy(h, k).wait_send()
        for copy in stores(h):
            copy.wait()
        return 0

    lax.fori_loop(0, heads, finish, 0)
    for stage in range(3):
        for copy in len_copies(stage):
            copy.wait_send()


def attention(prompts, live, q, g, kp, vp, kr, vr):
    vmem = pl.BlockSpec(memory_space=pltpu.VMEM)
    smem = pl.BlockSpec(memory_space=pltpu.SMEM)
    anywhere = pl.BlockSpec(memory_space=pl.ANY)
    heads, tokens, page = KEY_VALUE_HEADS, q.shape[0], kp.shape[0]
    plane = Z * Y * page
    total = CORES * plane + tokens
    lens = 6 + prompts - 1
    dma = pltpu.SemaphoreType.DMA
    return pl.pallas_call(
        functools.partial(kernel, prompts),
        out_shape=(
            jax.ShapeDtypeStruct(q.shape, BF16),
            jax.ShapeDtypeStruct(q.shape, BF16),
            jax.ShapeDtypeStruct(kr.shape, BF16),
            jax.ShapeDtypeStruct(kr.shape, BF16),
            jax.ShapeDtypeStruct(kp.shape, BF16),
            jax.ShapeDtypeStruct(kp.shape, BF16),
        ),
        in_specs=[smem] + [anywhere] * 6,
        out_specs=(anywhere, anywhere, vmem, vmem, vmem, vmem),
        scratch_shapes=[
            pltpu.VMEM((heads, 2, total, D), BF16),
            pltpu.VMEM(q.shape, BF16),
            pltpu.VMEM(q.shape, BF16),
            pltpu.VMEM(q.shape, BF16),
            pltpu.VMEM(q.shape, BF16),
            pltpu.VMEM((4, 2, total, D), F32),
            pltpu.VMEM((heads, 2, plane, D), BF16),
            pltpu.VMEM((heads, 2, plane, D), BF16),
            pltpu.VMEM((heads, 2, 2, page, D), BF16),
            pltpu.VMEM((heads, 2, 2, page, D), BF16),
            pltpu.VMEM((heads, 2, 2, Y * page, D), BF16),
            pltpu.VMEM((heads, 2, 2, Y * page, D), BF16),
            pltpu.VMEM((heads, 2, page, D), BF16),
            pltpu.VMEM((heads, 2, page, D), BF16),
            pltpu.VMEM((3, 8, D), F32),
            pltpu.VMEM((lens, 8, D), F32),
            pltpu.VMEM((8, D), F32),
            dma((heads, 6)),
            dma((heads, 2)),
            dma((heads, 12)),
            dma((heads, 12)),
            dma((heads, 6)),
            dma((heads, 6)),
            dma((lens,)),
            dma((lens,)),
        ],
        compiler_params=pltpu.CompilerParams(
            collective_id=0, has_side_effects=True, vmem_limit_bytes=60 * 2**20
        ),
        name="attention",
    )(live, q, g, kp, vp, kr, vr)


def shards(q, kr, vr, kp, vp, g, lengths):
    att, dq, dkr, dvr, pk, pv = attention(
        lax.axis_size("prompt"), lengths, q[0, 0], g[0, 0], kp[0], vp[0], kr[0, 0], vr[0, 0]
    )
    return att[None, None], dq[None, None], dkr[None, None], dvr[None, None], pk[None], pv[None]


def solution(mesh):
    four = P("prompt", "resp", None, None)
    three = P("prompt", "resp", None)
    return jax.shard_map(
        shards,
        mesh=mesh,
        in_specs=(four, four, four, three, three, four, P("prompt", "resp")),
        out_specs=(four, four, four, four, three, three),
        check_vma=False,
    )
```

time: 203 us -> 101 us (0.50)
  blocking collectives: 69.2 us -> 0 us
  waiting for transfers between devices: 64.1 us -> 0 us
  Pallas kernels: 43.7 us -> 90.1 us
  between operations: 15.4 us -> 1.31 us
    psum x1 -> x0, blocking collectives: 69.2 us -> none  [shards(): total = lax.psum(jnp.sum(lengths.astype(F32)), ('prompt', 'resp'))]
    reduce_scatter x1 -> x0, waiting for transfers between devices: 64 us -> none  [shards(): mine = lax.psum_scatter(dkv, 'resp', scatter_dimension=2, tiled=True)]
    pallas_call x1, Pallas kernels: 43.7 us -> 90.1 us  [attention(): pl.pallas_call(functools.partial(kernel, prompts), out_shape=(jax.ShapeDt...]
    unnamed x1 -> x16, local copies, waits for them, and re-layouts: 0.99 us -> 7.3 us
    slice x2 -> x0, local copies, waits for them, and re-layouts: 5.37 us -> none  [the longest x1 4.63 us: shards(): kv[:, width:]]
  transfers between devices with their start and end apart: 2 -> 0, of which waited for: 1 -> 0; matrix products, arithmetic and copies ran while one was open for 0% -> 0% of each run, Pallas kernels for 0% -> 0%
where the time goes in v2:
time: 101 us; the launch traced here: 98.7 us
  Pallas kernels  90.1 us (89%)
  local copies, waits for them, and re-layouts  7.3 us (7%)
  between operations  1.31 us (1%)
    pallas_call x1, Pallas kernels, attention(): pl.pallas_call(functools.partial(kernel, prompts), out_shape=(jax.ShapeDt...  90.1 us
    unnamed x16, local copies, waits for them, and re-layouts  7.3 us

profile of v2, /device:TPU:1, one launch (start us, length us, event | category | flops | bytes accessed | tf_op | source)
XLA Modules:
  0.0 98.7 jit_solution(12924984489547477313)
XLA Ops:
  1.3 90.1 %attention.1 = (bf16[128,8192]{1,0:T(8,128)(2,1)}, bf16[128,8192]{1,0:T(8,128)(2,1)}, bf16[128,1024]{1,0:T(8,128)(2,1)}, bf16[128,1024]{1,0:T(8,128)(2,1)}, bf16...) custom-call(s32[1,1]{1,0:T(1,128)S(6)} %copy.19.live_ref, bf16[128,8192]{1,0:T(8,128)(2,1)} %bitcast.12, ...), custom_call_target="tpu_custom_call" | custom-call | tf_op jit(solution)/shard_map/attention/pallas_call | solution.py:345
  91.4 0.0 copy-start
  91.4 3.2 %copy.20 = bf16[1,1,128,8192]{3,2,1,0:T(8,128)(2,1)} copy(bf16[1,1,128,8192]{3,2,1,0:T(8,128)(2,1)} %bitcast.15) | data formatting | bytes 4194304
  94.7 0.0 copy-done
  94.7 0.0 copy-start.2
  94.7 0.0 copy-start.1
  94.7 0.0 copy-start.4
  94.7 0.0 copy-start.3
  94.7 1.3 %copy.21 = bf16[1,1,128,8192]{3,2,1,0:T(8,128)(2,1)} copy(bf16[1,1,128,8192]{3,2,1,0:T(8,128)(2,1)S(1)} %bitcast.14) | data formatting | bytes 4194304
  96.0 0.0 copy-done.2
  96.0 0.7 copy.22
  96.7 0.0 copy-done.1
  96.7 0.7 copy.23
  97.4 0.0 copy-done.4
  97.4 0.7 copy.24
  98.1 0.0 copy-done.3
  98.1 0.7 copy.25
Async XLA Ops:
  91.4 3.3 %copy-start = (bf16[128,8192]{1,0:T(8,128)(2,1)S(1)}, bf16[128,8192]{1,0:T(8,128)(2,1)}, u32[]{:S(2)}) copy-start(bf16[128,8192]{1,0:T(8,128)(2,1)} %get-tuple-element.13) | copy-start | bytes 6291460
  94.7 1.3 %copy-start.2 = (bf16[128,1024]{1,0:T(8,128)(2,1)S(1)}, bf16[128,1024]{1,0:T(8,128)(2,1)}, u32[]{:S(2)}) copy-start(bf16[128,1024]{1,0:T(8,128)(2,1)} %get-tuple-element.14) | copy-start | bytes 786436
  94.7 2.0 %copy-start.1 = (bf16[128,1024]{1,0:T(8,128)(2,1)S(1)}, bf16[128,1024]{1,0:T(8,128)(2,1)}, u32[]{:S(2)}) copy-start(bf16[128,1024]{1,0:T(8,128)(2,1)} %get-tuple-element.15) | copy-start | bytes 786436
  94.7 2.8 %copy-start.4 = (bf16[64,1024]{1,0:T(8,128)(2,1)S(1)}, bf16[64,1024]{1,0:T(8,128)(2,1)}, u32[]{:S(2)}) copy-start(bf16[64,1024]{1,0:T(8,128)(2,1)} %get-tuple-element.16) | copy-start | bytes 393220
  94.7 3.4 %copy-start.3 = (bf16[64,1024]{1,0:T(8,128)(2,1)S(1)}, bf16[64,1024]{1,0:T(8,128)(2,1)}, u32[]{:S(2)}) copy-start(bf16[64,1024]{1,0:T(8,128)(2,1)} %get-tuple-element.17) | copy-start | bytes 393220

commit v3 on v2

v3 whole, which is shorter than its diff:
```python
import functools

import jax
import jax.numpy as jnp
from jax import lax
from jax.experimental import pallas as pl
from jax.experimental.pallas import tpu as pltpu
from jax.sharding import PartitionSpec as P

F32, BF16 = jnp.float32, jnp.bfloat16
QUERY_HEADS = 64
KEY_VALUE_HEADS = 8
GROUP = QUERY_HEADS // KEY_VALUE_HEADS
D = 128
INV = 1.0 / D**0.5
LOG2E = 1.4426950408889634
BLOCK_HEADS = 4
LAG = 4
Z, Y, CORES = 4, 2, 2
MESH = pl.DeviceIdType.MESH


def dot(a, b, ca, cb):
    return lax.dot_general(a, b, (((ca,), (cb,)), ((), ())), preferred_element_type=F32)


def kernel(
    prompts, live_ref, q_hbm, g_hbm, kp_hbm, vp_hbm, kr_hbm, vr_hbm,
    att_hbm, dq_hbm, dkr_ref, dvr_ref, pk_ref, pv_ref,
    kv, q_ref, g_ref, att_ref, dq_ref, grad,
    pair_out, pair_in, page_out, key_in, value_in, key_out2, key_in2, value_out2, value_in2, page_in, keep,
    ds_ref, scale_ref,
    lens_out, lens_in, factor_ref,
    load_sem, store_sem, ag_send, ag_recv, pair_send, pair_recv, rs_send, rs_recv,
    direct_send, direct_recv, len_send, len_recv,
):
    heads = KEY_VALUE_HEADS
    tokens = q_ref.shape[0]
    page = kp_hbm.shape[0]
    plane = Z * Y * page
    plen = CORES * plane
    me = lax.axis_index("resp")
    prompt = lax.axis_index("prompt")
    z, y, c = me // (Y * CORES), (me // CORES) % Y, me % CORES
    steps = (2, 1, 3)

    def place(zz, yy, cc):
        return {"resp": (zz * Y + yy) * CORES + cc}

    def ahead(i):
        return (z + steps[i]) % Z

    def behind(i):
        return (z + Z - steps[i]) % Z

    beside = place(z, 1 - y, c)
    sibling = place(z, y, 1 - c)
    len_peers = [
        [sibling],
        [beside],
        [place(ahead(i), y, c) for i in range(3)],
        [{"prompt": (prompt + k) % prompts} for k in range(2, prompts, 2)],
        [{"prompt": prompt + 1 - 2 * (prompt % 2)}],
    ]
    slots = [0, 1, 2, 5, 5 + prompts // 2 - 1]

    def page_rows(cc, zz, yy):
        return pl.ds(pl.multiple_of(cc * plane + (zz * Y + yy) * page, page), page)

    def plane_rows(cc):
        return pl.ds(pl.multiple_of(cc * plane, plane), plane)

    def columns(h):
        return pl.ds(pl.multiple_of(h * D, D), D)

    def block(h):
        return pl.ds(pl.multiple_of(h * GROUP * D, GROUP * D), GROUP * D)

    def load(h, i):
        mine, extra = page_rows(c, z, y), pl.ds(plen, tokens)
        src, dst = [
            lambda: (kp_hbm.at[:, columns(h)], kv.at[h, 0, mine, :]),
            lambda: (vp_hbm.at[:, columns(h)], kv.at[h, 1, mine, :]),
            lambda: (kr_hbm.at[:, columns(h)], kv.at[h, 0, extra, :]),
            lambda: (vr_hbm.at[:, columns(h)], kv.at[h, 1, extra, :]),
            lambda: (q_hbm.at[:, block(h)], q_ref.at[:, block(h)]),
            lambda: (g_hbm.at[:, block(h)], g_ref.at[:, block(h)]),
        ][i]()
        return pltpu.make_async_copy(src, dst, load_sem.at[h, i])

    def store(h, i):
        src, dst = [lambda: (att_ref, att_hbm), lambda: (dq_ref, dq_hbm)][i]()
        return pltpu.make_async_copy(src.at[:, block(h)], dst.at[:, block(h)], store_sem.at[h, i])

    def gather_copy(h, k, part, rows, to):
        piece = kv.at[h, part, rows, :]
        return pltpu.make_async_remote_copy(
            piece, piece, ag_send.at[h, k], ag_recv.at[h, k], device_id=to, device_id_type=MESH
        )

    both = slice(None)

    def gather_start(h):
        mine = page_rows(c, z, y)
        for i in range(2):
            load(h, i).wait()
        for i in range(3):
            gather_copy(h, i, both, mine, place(ahead(i), y, c)).start()
        gather_copy(h, 3, both, mine, beside).start()

    def gather_direct(h):
        mine = page_rows(c, z, y)
        for part in range(2):
            for i in range(3):
                gather_copy(h, 4 + 3 * part + i, part, mine, place(ahead(i), 1 - y, c)).start()

    def gather_wait(h):
        gather_copy(h, 3, both, page_rows(c, z, 1 - y), beside).wait_recv()
        for i in range(3):
            gather_copy(h, i, both, page_rows(c, behind(i), y), place(behind(i), y, c)).wait_recv()

    def gather_pass(h):
        gather_wait(h)
        for i in range(3):
            gather_copy(h, 4 + i, 0, page_rows(c, z, 1 - y), place(ahead(i), y, c)).start()
        for i in range(3):
            gather_copy(h, 7 + i, 1, page_rows(c, behind(i), y), beside).start()

    def gather_share(h):
        for part in range(2):
            for i in range(3):
                rows = page_rows(c, behind(i), 1 - y)
                gather_copy(h, 4 + 3 * part + i, part, rows, beside).wait_recv()
            gather_copy(h, 10 + part, part, plane_rows(c), sibling).start()

    def gathered(h):
        for part in range(2):
            gather_copy(h, 10 + part, part, plane_rows(1 - c), sibling).wait_recv()
        for i in range(2, 6):
            load(h, i).wait()

    def gather_sent(h):
        mine = page_rows(c, z, y)
        for k in range(12):
            part = both if k < 4 else (k - 4) // 3 if k < 10 else k - 10
            gather_copy(h, k, part, mine if k < 10 else plane_rows(c), sibling).wait_send()

    def pair_copy(h):
        return pltpu.make_async_remote_copy(
            pair_out.at[h], pair_in.at[h], pair_send.at[h], pair_recv.at[h],
            device_id=sibling, device_id_type=MESH,
        )

    def sum_copy(h, k):
        i = k if k < 3 else k - 5
        src, dst = [
            lambda: (page_out.at[h, 0, ahead(i)], key_in.at[h, i]),
            lambda: (page_out.at[h, 1, :, 1 - y], value_in.at[h]),
            lambda: (key_out2.at[h], key_in2.at[h]),
            lambda: (value_out2.at[h, ahead(i)], value_in2.at[h, i]),
        ][0 if k < 3 else k - 2 if k < 5 else 3]()
        to = beside if k in (3, 4) else place(ahead(i), y, c)
        return pltpu.make_async_remote_copy(
            src, dst, rs_send.at[h, k], rs_recv.at[h, k], device_id=to, device_id_type=MESH
        )

    def direct_copy(k):
        dz, dy = [(2, 1), (2, 0), (1, 1), (3, 1), (1, 0), (3, 0), (0, 1)][k]
        zz, yy = (z + dz) % Z, (y + dy) % Y
        return pltpu.make_async_remote_copy(
            page_out.at[heads - 1, :, zz, yy], page_in.at[k], direct_send.at[k], direct_recv.at[k],
            device_id=place(zz, yy, c), device_id_type=MESH,
        )

    def sum0(h):
        pair_out[h] = grad[h % 4, :, plane_rows(1 - c), :].astype(BF16)
        pair_copy(h).start()

    def sum_pair(h):
        pair_copy(h).wait_recv()
        total = grad[h % 4, :, plane_rows(c), :] + pair_in[h].astype(F32)
        page_out[h] = total.astype(BF16).reshape(page_out.shape[1:])

    def sum1(h):
        sum_pair(h)
        for k in range(4):
            sum_copy(h, k).start()

    def own(h, part, zz, yy):
        return grad[h % 4, part, page_rows(c, zz, yy), :] + pair_in[h, part, page_rows(0, zz, yy), :].astype(F32)

    def sum2(h):
        mine, other = own(h, 0, z, y), own(h, 0, z, 1 - y)
        for k in range(3):
            sum_copy(h, k).wait_recv()
            mine = mine + key_in[h, k, y].astype(F32)
            other = other + key_in[h, k, 1 - y].astype(F32)
        keep[h % 4, 0] = mine
        key_out2[h] = other.astype(BF16)
        sum_copy(h, 4).start()
        sum_copy(h, 3).wait_recv()
        for i in range(3):
            value_out2[h, ahead(i)] = (own(h, 1, ahead(i), y) + value_in[h, ahead(i)].astype(F32)).astype(BF16)
            sum_copy(h, 5 + i).start()
        keep[h % 4, 1] = own(h, 1, z, y) + value_in[h, z].astype(F32)

    def put(h, dk, dv):
        factor = factor_ref[0:1, :]
        pk_ref[:, columns(h)] = (dk * (factor * INV)).astype(BF16)
        pv_ref[:, columns(h)] = (dv * factor).astype(BF16)

    def sum3(h):
        sum_copy(h, 4).wait_recv()
        dk, dv = keep[h % 4, 0] + key_in2[h].astype(F32), keep[h % 4, 1]
        for i in range(3):
            sum_copy(h, 5 + i).wait_recv()
            dv = dv + value_in2[h, i].astype(F32)
        put(h, dk, dv)

    def direct1():
        sum_pair(heads - 1)
        for k in range(7):
            direct_copy(k).start()

    def direct2():
        dk, dv = own(heads - 1, 0, z, y), own(heads - 1, 1, z, y)
        for k in range(7):
            direct_copy(k).wait_recv()
            dk = dk + page_in[k, 0].astype(F32)
            dv = dv + page_in[k, 1].astype(F32)
        put(heads - 1, dk, dv)

    def len_slot(stage, i):
        return slots[stage] + i

    def len_copies(stage):
        return [
            pltpu.make_async_remote_copy(
                lens_out.at[stage], lens_in.at[len_slot(stage, i)],
                len_send.at[len_slot(stage, i)], len_recv.at[len_slot(stage, i)],
                device_id=peer, device_id_type=MESH,
            )
            for i, peer in enumerate(len_peers[stage])
        ]

    def len_start(stage):
        for copy in len_copies(stage):
            copy.start()

    def len_sum(stage):
        total = lens_out[stage]
        for i, copy in enumerate(len_copies(stage)):
            copy.wait_recv()
            total = total + lens_in[len_slot(stage, i)]
        return total

    def len_next(stage):
        lens_out[stage + 1] = len_sum(stage)
        len_start(stage + 1)

    def set_factor():
        factor_ref[...] = (prompts * Z * Y * CORES * tokens) / len_sum(4)

    rows = BLOCK_HEADS * tokens
    live = live_ref[0, 0]

    def first(h, j, keys, values):
        cols = [columns(h * GROUP + j * BLOCK_HEADS + i) for i in range(BLOCK_HEADS)]
        token = lax.broadcasted_iota(jnp.int32, (rows, 1), 0) % tokens
        q = jnp.concatenate([q_ref[:, k] for k in cols], 0)
        g = jnp.concatenate([g_ref[:, k] for k in cols], 0)
        g = jnp.where(token < live, g.astype(F32), 0.0).astype(BF16)
        return q, g, dot(q, keys, 1, 1), dot(g, values, 1, 1)

    def rest(h, j, values, state, totals):
        q, g, s, dp = state
        cols = [columns(h * GROUP + j * BLOCK_HEADS + i) for i in range(BLOCK_HEADS)]
        token = lax.broadcasted_iota(jnp.int32, (rows, tokens), 0) % tokens
        key = lax.broadcasted_iota(jnp.int32, (rows, tokens), 1)
        s = jnp.concatenate([s[:, :plen], jnp.where(key <= token, s[:, plen:], -1e30)], 1)
        top = jnp.max(s, 1, keepdims=True)
        e = jnp.exp2(s * (INV * LOG2E) - top * (INV * LOG2E))
        scale = 1.0 / jnp.sum(e, 1, keepdims=True)
        e = e.astype(BF16)
        o = dot(e, values, 1, 0) * scale
        for i, k in enumerate(cols):
            att_ref[:, k] = o[i * tokens : (i + 1) * tokens].astype(BF16)
        gf = g.astype(F32)
        delta = jnp.sum(gf * o, 1, keepdims=True)
        ds = e * (dp - delta).astype(BF16)
        g = (gf * scale).astype(BF16)
        q = (q.astype(F32) * scale).astype(BF16)
        dk, dv = dot(q.T, ds, 1, 0), dot(g.T, e, 1, 0)
        totals = (dk, dv) if totals is None else (totals[0] + dk, totals[1] + dv)
        place_rows = pl.ds(j * rows, rows)
        ds_ref[h % LAG, place_rows, :] = ds
        scale_ref[h % LAG, place_rows, :] = jnp.broadcast_to(scale * INV, (rows, D))
        return totals

    def query_grad(h, j, keys):
        cols = [columns(h * GROUP + j * BLOCK_HEADS + i) for i in range(BLOCK_HEADS)]
        place_rows = pl.ds(j * rows, rows)
        dq = dot(ds_ref[h % LAG, place_rows, :], keys, 1, 0)
        dq = dq * (scale_ref[h % LAG, place_rows, :] * factor_ref[0:1, :])
        for i, k in enumerate(cols):
            dq_ref[:, k] = dq[i * tokens : (i + 1) * tokens].astype(BF16)

    def resp_put(h):
        factor = factor_ref[0:1, :]
        dkr_ref[:, columns(h)] = (grad[h % 4, 0, plen:, :] * (factor * INV)).astype(BF16)
        dvr_ref[:, columns(h)] = (grad[h % 4, 1, plen:, :] * factor).astype(BF16)

    def when(condition, stage, h):
        pl.when(condition)(functools.partial(stage, h))

    def head(lagging, h, _):
        gathered(h)
        keys, values = kv[h, 0], kv[h, 1]
        blocks = GROUP // BLOCK_HEADS
        state, totals = first(h, 0, keys, values), None
        for j in range(blocks):
            after = first(h, j + 1, keys, values) if j + 1 < blocks else None
            if lagging:
                query_grad(h - LAG, j, kv[h - LAG, 0])
            totals = rest(h, j, values, state, totals)
            state = after
            if j == 0:
                for stage in range(1, 4):
                    pl.when(h == stage - 1)(functools.partial(len_next, stage))
                pl.when(h == 3)(set_factor)
                when(h + 3 < heads, gather_start, h + 3)
                when(h >= 1, sum1, h - 1)
                when(h + 2 < heads, gather_pass, h + 2)
                when(h + 1 < heads, gather_share, h + 1)
                when(h >= 2, sum2, h - 2)
                when(h >= 3, sum3, h - 3)
                when(h >= 3, resp_put, h - 3)
        grad[h % 4, 0] = totals[0].T
        grad[h % 4, 1] = totals[1].T
        sum0(h)
        store(h, 0).start()
        if lagging:
            store(h - LAG, 1).start()
        return 0

    def start_loads(h, _):
        for i in range(6):
            load(h, i).start()
        return 0

    lax.fori_loop(0, heads, start_loads, 0)
    lens_out[0] = jnp.full(lens_out.shape[1:], live.astype(F32))
    barrier = pltpu.get_barrier_semaphore()
    peers = [p for stage in len_peers for p in stage] + [place(ahead(i), 1 - y, c) for i in range(3)]
    for p in peers:
        pl.semaphore_signal(barrier, inc=1, device_id=p, device_id_type=MESH)
    pl.semaphore_wait(barrier, len(peers))

    for h in range(2):
        gather_start(h)
        gather_direct(h)
    len_start(0)
    gather_start(2)
    gather_wait(0)
    gather_share(0)
    len_next(0)
    gather_wait(1)

    lax.fori_loop(0, LAG, functools.partial(head, False), 0)
    lax.fori_loop(LAG, heads, functools.partial(head, True), 0)

    direct1()
    for h in range(heads - LAG, heads):
        keys = kv[h, 0]
        for j in range(GROUP // BLOCK_HEADS):
            query_grad(h, j, keys)
        store(h, 1).start()
        if h == heads - 2:
            sum2(heads - 2)
    for h in range(heads - 3, heads):
        resp_put(h)
    sum3(heads - 3)
    sum3(heads - 2)
    direct2()

    def finish(h, _):
        gather_sent(h)
        pair_copy(h).wait_send()
        for i in range(2):
            store(h, i).wait()
        return 0

    def summed(h, _):
        for k in range(8):
            sum_copy(h, k).wait_send()
        return 0

    lax.fori_loop(0, heads, finish, 0)
    lax.fori_loop(0, heads - 1, summed, 0)
    for k in range(7):
        direct_copy(k).wait_send()
    for stage in range(5):
        for copy in len_copies(stage):
            copy.wait_send()


def attention(prompts, live, q, g, kp, vp, kr, vr):
    vmem = pl.BlockSpec(memory_space=pltpu.VMEM)
    smem = pl.BlockSpec(memory_space=pltpu.SMEM)
    anywhere = pl.BlockSpec(memory_space=pl.ANY)
    heads, tokens, page = KEY_VALUE_HEADS, q.shape[0], kp.shape[0]
    plane = Z * Y * page
    total = CORES * plane + tokens
    lens = 6 + prompts // 2 - 1
    dma = pltpu.SemaphoreType.DMA
    return pl.pallas_call(
        functools.partial(kernel, prompts),
        out_shape=(
            jax.ShapeDtypeStruct(q.shape, BF16),
            jax.ShapeDtypeStruct(q.shape, BF16),
            jax.ShapeDtypeStruct(kr.shape, BF16),
            jax.ShapeDtypeStruct(kr.shape, BF16),
            jax.ShapeDtypeStruct(kp.shape, BF16),
            jax.ShapeDtypeStruct(kp.shape, BF16),
        ),
        in_specs=[smem] + [anywhere] * 6,
        out_specs=(anywhere, anywhere, vmem, vmem, vmem, vmem),
        scratch_shapes=[
            pltpu.VMEM((heads, 2, total, D), BF16),
            pltpu.VMEM(q.shape, BF16),
            pltpu.VMEM(q.shape, BF16),
            pltpu.VMEM(q.shape, BF16),
            pltpu.VMEM(q.shape, BF16),
            pltpu.VMEM((4, 2, total, D), F32),
            pltpu.VMEM((heads, 2, plane, D), BF16),
            pltpu.VMEM((heads, 2, plane, D), BF16),
            pltpu.VMEM((heads, 2, Z, Y, page, D), BF16),
            pltpu.VMEM((heads, 3, Y, page, D), BF16),
            pltpu.VMEM((heads, Z, page, D), BF16),
            pltpu.VMEM((heads, page, D), BF16),
            pltpu.VMEM((heads, page, D), BF16),
            pltpu.VMEM((heads, Z, page, D), BF16),
            pltpu.VMEM((heads, 3, page, D), BF16),
            pltpu.VMEM((7, 2, page, D), BF16),
            pltpu.VMEM((4, 2, page, D), F32),
            pltpu.VMEM((LAG, GROUP * tokens, total), BF16),
            pltpu.VMEM((LAG, GROUP * tokens, D), F32),
            pltpu.VMEM((5, 8, D), F32),
            pltpu.VMEM((lens, 8, D), F32),
            pltpu.VMEM((8, D), F32),
            dma((heads, 6)),
            dma((heads, 2)),
            dma((heads, 12)),
            dma((heads, 12)),
            dma((heads,)),
            dma((heads,)),
            dma((heads, 8)),
            dma((heads, 8)),
            dma((7,)),
            dma((7,)),
            dma((lens,)),
            dma((lens,)),
        ],
        compiler_params=pltpu.CompilerParams(
            collective_id=0, has_side_effects=True, vmem_limit_bytes=60 * 2**20
        ),
        name="attention",
    )(live, q, g, kp, vp, kr, vr)


def write_kernel(*refs):
    n = len(refs) // 3
    ins, outs, held = refs[:n], refs[n : 2 * n], refs[2 * n : 3 * n]
    read_sem, write_sem = refs[3 * n :]
    parts = []
    for a, b, v in zip(ins, outs, held):
        count = max(1, a.shape[1] // 2048)
        width = a.shape[1] // count
        parts += [(a, b, v, pl.ds(i * width, width)) for i in range(count)]

    def copies(i):
        a, b, v, cols = parts[i]
        return (
            pltpu.make_async_copy(a.at[:, cols], v.at[:, cols], read_sem.at[i]),
            pltpu.make_async_copy(v.at[:, cols], b.at[:, cols], write_sem.at[i]),
        )

    pairs = [copies(i) for i in range(len(parts))]
    for read, _ in pairs:
        read.start()
    for read, write in pairs:
        read.wait()
        write.start()
    for _, write in pairs:
        write.wait()


def write_out(*arrays):
    anywhere = pl.BlockSpec(memory_space=pl.ANY)
    return pl.pallas_call(
        write_kernel,
        out_shape=tuple(jax.ShapeDtypeStruct(a.shape, a.dtype) for a in arrays),
        in_specs=[anywhere] * len(arrays),
        out_specs=(anywhere,) * len(arrays),
        scratch_shapes=[pltpu.VMEM(a.shape, a.dtype) for a in arrays]
        + [pltpu.SemaphoreType.DMA((16,)), pltpu.SemaphoreType.DMA((16,))],
        compiler_params=pltpu.CompilerParams(vmem_limit_bytes=60 * 2**20),
        name="write_out",
    )(*arrays)


def shards(q, kr, vr, kp, vp, g, lengths):
    att, dq, dkr, dvr, pk, pv = attention(
        lax.axis_size("prompt"), lengths, q[0, 0], g[0, 0], kp[0], vp[0], kr[0, 0], vr[0, 0]
    )
    att, dq, dkr, dvr, pk, pv = write_out(att, dq, dkr, dvr, pk, pv)
    return att[None, None], dq[None, None], dkr[None, None], dvr[None, None], pk[None], pv[None]


def solution(mesh):
    four = P("prompt", "resp", None, None)
    three = P("prompt", "resp", None)
    return jax.shard_map(
        shards,
        mesh=mesh,
        in_specs=(four, four, four, three, three, four, P("prompt", "resp")),
        out_specs=(four, four, four, four, three, three),
        check_vma=False,
    )
```

time: 101 us -> 76 us (0.75); the launches traced: 98.7 us -> 75.9 us
  Pallas kernels: 90.1 us -> 74.4 us
  local copies, waits for them, and re-layouts: 7.3 us -> 0 us
    pallas_call x1, Pallas kernels: 90.1 us -> 70 us  [attention(): pl.pallas_call(functools.partial(kernel, prompts), out_shape=(jax.ShapeDt...]
    unnamed x16 -> x0, local copies, waits for them, and re-layouts: 7.3 us -> none
    pallas_call x0 -> x1, Pallas kernels: none -> 4.42 us  [write_out(): pl.pallas_call(write_kernel, out_shape=tuple((jax.ShapeDtypeStruct(a.shap...]
where the time goes in v3:
time: 76 us; the launch traced here: 75.9 us
  Pallas kernels  74.4 us (98%)
  between operations  1.45 us (2%)
    pallas_call x1, Pallas kernels, attention(): pl.pallas_call(functools.partial(kernel, prompts), out_shape=(jax.ShapeDt...  70 us
    pallas_call x1, Pallas kernels, write_out(): pl.pallas_call(write_kernel, out_shape=tuple((jax.ShapeDtypeStruct(a.shap...  4.42 us

profile of v3, /device:TPU:1, one launch (start us, length us, event | category | flops | bytes accessed | tf_op | source)
XLA Modules:
  0.0 75.9 jit_solution(6744741706144209782)
XLA Ops:
  1.3 70.0 %attention.1 = (bf16[128,8192]{1,0:T(8,128)(2,1)}, bf16[128,8192]{1,0:T(8,128)(2,1)}, bf16[128,1024]{1,0:T(8,128)(2,1)}, bf16[128,1024]{1,0:T(8,128)(2,1)}, bf16...) custom-call(s32[1,1]{1,0:T(1,128)S(6)} %copy.13.live_ref, bf16[128,8192]{1,0:T(8,128)(2,1)} %bitcast.12, ...), custom_call_target="tpu_custom_call" | custom-call | tf_op jit(solution)/shard_map/attention/pallas_call | solution.py:416
  71.3 4.4 %write_out.1 = (bf16[128,8192]{1,0:T(8,128)(2,1)}, bf16[128,8192]{1,0:T(8,128)(2,1)}, bf16[128,1024]{1,0:T(8,128)(2,1)}, bf16[128,1024]{1,0:T(8,128)(2,1)}, bf16...) custom-call(bf16[128,8192]{1,0:T(8,128)(2,1)} %get-tuple-element.18.refs_0_, bf16[128,8192]{1,0:T(8,128)(2,1)} %get-tuple-element.19.refs_1_, ...), custom_call_target="tpu_custom_call" | custom-call | tf_op jit(solution)/shard_map/write_out/pallas_call | solution.py:500

commit v4 on v3

--- a/solution.py
+++ b/solution.py
@@ -26,13 +26,13 @@
 
 def kernel(
     prompts, live_ref, q_hbm, g_hbm, kp_hbm, vp_hbm, kr_hbm, vr_hbm,
-    att_hbm, dq_hbm, dkr_ref, dvr_ref, pk_ref, pv_ref,
-    kv, q_ref, g_ref, att_ref, dq_ref, grad,
+    att_ref, dq_ref, dkr_ref, dvr_ref, pk_ref, pv_ref,
+    kv, q_ref, g_ref, grad,
     pair_out, pair_in, page_out, key_in, value_in, key_out2, key_in2, value_out2, value_in2, page_in, keep,
     ds_ref, scale_ref,
     lens_out, lens_in, factor_ref,
-    load_sem, store_sem, ag_send, ag_recv, pair_send, pair_recv, rs_send, rs_recv,
-    direct_send, direct_recv, len_send, len_recv,
+    load_sem, ag_send, ag_recv, pair_send, pair_recv, rs_send, rs_recv,
+    direct_send, direct_recv, first_send, first_recv, len_send, len_recv,
 ):
     heads = KEY_VALUE_HEADS
     tokens = q_ref.shape[0]
@@ -88,10 +88,6 @@
         ][i]()
         return pltpu.make_async_copy(src, dst, load_sem.at[h, i])
 
-    def store(h, i):
-        src, dst = [lambda: (att_ref, att_hbm), lambda: (dq_ref, dq_hbm)][i]()
-        return pltpu.make_async_copy(src.at[:, block(h)], dst.at[:, block(h)], store_sem.at[h, i])
-
     def gather_copy(h, k, part, rows, to):
         piece = kv.at[h, part, rows, :]
         return pltpu.make_async_remote_copy(
@@ -133,16 +129,45 @@
                 gather_copy(h, 4 + 3 * part + i, part, rows, beside).wait_recv()
             gather_copy(h, 10 + part, part, plane_rows(c), sibling).start()
 
-    def gathered(h):
+    def gathered_keys(h):
+        gather_copy(h, 10, 0, plane_rows(1 - c), sibling).wait_recv()
+        for i in (2, 4):
+            load(h, i).wait()
+
+    def gathered_values(h):
+        gather_copy(h, 11, 1, plane_rows(1 - c), sibling).wait_recv()
+        for i in (3, 5):
+            load(h, i).wait()
+
+    def first_copy(part, k, rows, to):
+        if part == 0 or k > 3:
+            return gather_copy(0, k, part, rows, to)
+        piece = kv.at[0, 1, rows, :]
+        return pltpu.make_async_remote_copy(
+            piece, piece, first_send.at[k], first_recv.at[k], device_id=to, device_id_type=MESH
+        )
+
+    def first_start():
+        mine = page_rows(c, z, y)
         for part in range(2):
-            gather_copy(h, 10 + part, part, plane_rows(1 - c), sibling).wait_recv()
-        for i in range(2, 6):
-            load(h, i).wait()
-
-    def gather_sent(h):
+            load(0, part).wait()
+            for i in range(3):
+                first_copy(part, i, mine, place(ahead(i), y, c)).start()
+                first_copy(part, 4 + 3 * part + i, mine, place(ahead(i), 1 - y, c)).start()
+            first_copy(part, 3, mine, beside).start()
+
+    def first_share():
+        for part in range(2):
+            for i in range(3):
+                first_copy(part, i, page_rows(c, behind(i), y), beside).wait_recv()
+                first_copy(part, 4 + 3 * part + i, page_rows(c, behind(i), 1 - y), beside).wait_recv()
+            first_copy(part, 3, page_rows(c, z, 1 - y), beside).wait_recv()
+            gather_copy(0, 10 + part, part, plane_rows(c), sibling).start()
+
+    def gather_sent(h, whole=slice(None)):
         mine = page_rows(c, z, y)
         for k in range(12):
-            part = both if k < 4 else (k - 4) // 3 if k < 10 else k - 10
+            part = whole if k < 4 else (k - 4) // 3 if k < 10 else k - 10
             gather_copy(h, k, part, mine if k < 10 else plane_rows(c), sibling).wait_send()
 
     def pair_copy(h):
@@ -264,13 +289,14 @@
     rows = BLOCK_HEADS * tokens
     live = live_ref[0, 0]
 
-    def first(h, j, keys, values):
+    def first(h, j, keys):
         cols = [columns(h * GROUP + j * BLOCK_HEADS + i) for i in range(BLOCK_HEADS)]
         token = lax.broadcasted_iota(jnp.int32, (rows, 1), 0) % tokens
         q = jnp.concatenate([q_ref[:, k] for k in cols], 0)
+        s = dot(q, keys, 1, 1)
         g = jnp.concatenate([g_ref[:, k] for k in cols], 0)
         g = jnp.where(token < live, g.astype(F32), 0.0).astype(BF16)
-        return q, g, dot(q, keys, 1, 1), dot(g, values, 1, 1)
+        return q, g, s, dot(g, kv[h, 1], 1, 1)
 
     def rest(h, j, values, state, totals):
         q, g, s, dp = state
@@ -314,33 +340,31 @@
         pl.when(condition)(functools.partial(stage, h))
 
     def head(lagging, h, _):
-        gathered(h)
-        keys, values = kv[h, 0], kv[h, 1]
+        gathered_keys(h)
+        gathered_values(h)
+        for stage in range(1, 4):
+            pl.when(h == stage - 1)(functools.partial(len_next, stage))
+        pl.when(h == 3)(set_factor)
+        when(h + 3 < heads, gather_start, h + 3)
+        when(h >= 2, sum1, h - 2)
+        when((h >= 1) & (h + 2 < heads), gather_pass, h + 2)
+        when(h < 2, gather_wait, h + 1)
+        when(h >= 3, sum2, h - 3)
+        when(h >= 4, sum3, h - 4)
+        when(h >= 4, resp_put, h - 4)
+        when(h + 1 < heads, gather_share, h + 1)
+        keys = kv[h, 0]
         blocks = GROUP // BLOCK_HEADS
-        state, totals = first(h, 0, keys, values), None
+        state, totals = first(h, 0, keys), None
         for j in range(blocks):
-            after = first(h, j + 1, keys, values) if j + 1 < blocks else None
+            after = first(h, j + 1, keys) if j + 1 < blocks else None
             if lagging:
                 query_grad(h - LAG, j, kv[h - LAG, 0])
-            totals = rest(h, j, values, state, totals)
+            totals = rest(h, j, kv[h, 1], state, totals)
             state = after
-            if j == 0:
-                for stage in range(1, 4):
-                    pl.when(h == stage - 1)(functools.partial(len_next, stage))
-                pl.when(h == 3)(set_factor)
-                when(h + 3 < heads, gather_start, h + 3)
-                when(h >= 1, sum1, h - 1)
-                when(h + 2 < heads, gather_pass, h + 2)
-                when(h + 1 < heads, gather_share, h + 1)
-                when(h >= 2, sum2, h - 2)
-                when(h >= 3, sum3, h - 3)
-                when(h >= 3, resp_put, h - 3)
         grad[h % 4, 0] = totals[0].T
         grad[h % 4, 1] = totals[1].T
         sum0(h)
-        store(h, 0).start()
-        if lagging:
-            store(h - LAG, 1).start()
         return 0
 
     def start_loads(h, _):
@@ -348,60 +372,65 @@
             load(h, i).start()
         return 0
 
-    lax.fori_loop(0, heads, start_loads, 0)
-    lens_out[0] = jnp.full(lens_out.shape[1:], live.astype(F32))
     barrier = pltpu.get_barrier_semaphore()
     peers = [p for stage in len_peers for p in stage] + [place(ahead(i), 1 - y, c) for i in range(3)]
     for p in peers:
         pl.semaphore_signal(barrier, inc=1, device_id=p, device_id_type=MESH)
+    lax.fori_loop(0, heads, start_loads, 0)
+    lens_out[0] = jnp.full(lens_out.shape[1:], live.astype(F32))
     pl.semaphore_wait(barrier, len(peers))
 
-    for h in range(2):
+    first_start()
+    len_start(0)
+    for h in range(1, 3):
         gather_start(h)
         gather_direct(h)
-    len_start(0)
-    gather_start(2)
-    gather_wait(0)
-    gather_share(0)
+    first_share()
     len_next(0)
-    gather_wait(1)
 
     lax.fori_loop(0, LAG, functools.partial(head, False), 0)
     lax.fori_loop(LAG, heads, functools.partial(head, True), 0)
 
-    direct1()
-    for h in range(heads - LAG, heads):
-        keys = kv[h, 0]
+    def last_query_grad(h):
         for j in range(GROUP // BLOCK_HEADS):
-            query_grad(h, j, keys)
-        store(h, 1).start()
-        if h == heads - 2:
-            sum2(heads - 2)
-    for h in range(heads - 3, heads):
-        resp_put(h)
-    sum3(heads - 3)
-    sum3(heads - 2)
-    direct2()
+            query_grad(h, j, kv[h, 0])
 
     def finish(h, _):
         gather_sent(h)
+        return 0
+
+    def summed(h, _):
         pair_copy(h).wait_send()
-        for i in range(2):
-            store(h, i).wait()
-        return 0
-
-    def summed(h, _):
         for k in range(8):
             sum_copy(h, k).wait_send()
         return 0
 
-    lax.fori_loop(0, heads, finish, 0)
+    n = heads
+    sum1(n - 2)
+    sum2(n - 3)
+    last_query_grad(n - LAG)
+    direct1()
+    sum3(n - 4)
+    for h in range(n - 4, n):
+        resp_put(h)
+    for h in range(n - LAG + 1, n - 1):
+        last_query_grad(h)
+    sum2(n - 2)
+    sum3(n - 3)
+    last_query_grad(n - 1)
+    gather_sent(0, 0)
+    for k in range(4):
+        first_copy(1, k, page_rows(c, z, y), sibling).wait_send()
+    lax.fori_loop(1, heads, finish, 0)
     lax.fori_loop(0, heads - 1, summed, 0)
-    for k in range(7):
-        direct_copy(k).wait_send()
     for stage in range(5):
         for copy in len_copies(stage):
             copy.wait_send()
+    sum3(n - 2)
+    direct2()
+    pair_copy(n - 1).wait_send()
+    for k in range(7):
+        direct_copy(k).wait_send()
 
 
 def attention(prompts, live, q, g, kp, vp, kr, vr):
@@ -415,20 +444,11 @@
     dma = pltpu.SemaphoreType.DMA
     return pl.pallas_call(
         functools.partial(kernel, prompts),
-        out_shape=(
-            jax.ShapeDtypeStruct(q.shape, BF16),
-            jax.ShapeDtypeStruct(q.shape, BF16),
-            jax.ShapeDtypeStruct(kr.shape, BF16),
-            jax.ShapeDtypeStruct(kr.shape, BF16),
-            jax.ShapeDtypeStruct(kp.shape, BF16),
-            jax.ShapeDtypeStruct(kp.shape, BF16),
-        ),
+        out_shape=tuple(pltpu.VMEM(a.shape, BF16) for a in (q, q, kr, kr, kp, kp)),
         in_specs=[smem] + [anywhere] * 6,
-        out_specs=(anywhere, anywhere, vmem, vmem, vmem, vmem),
+        out_specs=(vmem,) * 6,
         scratch_shapes=[
             pltpu.VMEM((heads, 2, total, D), BF16),
-            pltpu.VMEM(q.shape, BF16),
-            pltpu.VMEM(q.shape, BF16),
             pltpu.VMEM(q.shape, BF16),
             pltpu.VMEM(q.shape, BF16),
             pltpu.VMEM((4, 2, total, D), F32),
@@ -449,7 +469,6 @@
             pltpu.VMEM((lens, 8, D), F32),
             pltpu.VMEM((8, D), F32),
             dma((heads, 6)),
-            dma((heads, 2)),
             dma((heads, 12)),
             dma((heads, 12)),
             dma((heads,)),
@@ -458,62 +477,22 @@
             dma((heads, 8)),
             dma((7,)),
             dma((7,)),
+            dma((4,)),
+            dma((4,)),
             dma((lens,)),
             dma((lens,)),
         ],
         compiler_params=pltpu.CompilerParams(
-            collective_id=0, has_side_effects=True, vmem_limit_bytes=60 * 2**20
+            collective_id=0, has_side_effects=True, vmem_limit_bytes=59 * 2**20
         ),
         name="attention",
     )(live, q, g, kp, vp, kr, vr)
-
-
-def write_kernel(*refs):
-    n = len(refs) // 3
-    ins, outs, held = refs[:n], refs[n : 2 * n], refs[2 * n : 3 * n]
-    read_sem, write_sem = refs[3 * n :]
-    parts = []
-    for a, b, v in zip(ins, outs, held):
-        count = max(1, a.shape[1] // 2048)
-        width = a.shape[1] // count
-        parts += [(a, b, v, pl.ds(i * width, width)) for i in range(count)]
-
-    def copies(i):
-        a, b, v, cols = parts[i]
-        return (
-            pltpu.make_async_copy(a.at[:, cols], v.at[:, cols], read_sem.at[i]),
-            pltpu.make_async_copy(v.at[:, cols], b.at[:, cols], write_sem.at[i]),
-        )
-
-    pairs = [copies(i) for i in range(len(parts))]
-    for read, _ in pairs:
-        read.start()
-    for read, write in pairs:
-        read.wait()
-        write.start()
-    for _, write in pairs:
-        write.wait()
-
-
-def write_out(*arrays):
-    anywhere = pl.BlockSpec(memory_space=pl.ANY)
-    return pl.pallas_call(
-        write_kernel,
-        out_shape=tuple(jax.ShapeDtypeStruct(a.shape, a.dtype) for a in arrays),
-        in_specs=[anywhere] * len(arrays),
-        out_specs=(anywhere,) * len(arrays),
-        scratch_shapes=[pltpu.VMEM(a.shape, a.dtype) for a in arrays]
-        + [pltpu.SemaphoreType.DMA((16,)), pltpu.SemaphoreType.DMA((16,))],
-        compiler_params=pltpu.CompilerParams(vmem_limit_bytes=60 * 2**20),
-        name="write_out",
-    )(*arrays)
 
 
 def shards(q, kr, vr, kp, vp, g, lengths):
     att, dq, dkr, dvr, pk, pv = attention(
         lax.axis_size("prompt"), lengths, q[0, 0], g[0, 0], kp[0], vp[0], kr[0, 0], vr[0, 0]
     )
-    att, dq, dkr, dvr, pk, pv = write_out(att, dq, dkr, dvr, pk, pv)
     return att[None, None], dq[None, None], dkr[None, None], dvr[None, None], pk[None], pv[None]
 
 

time: 76 us -> 72.7 us (0.957)
  Pallas kernels: 74.4 us -> 65.9 us
  local copies, waits for them, and re-layouts: 0 us -> 5.35 us
    pallas_call x2 -> x1, Pallas kernels: 74.4 us -> 65.9 us  [attention(): pl.pallas_call(functools.partial(kernel, prompts), out_shape=tuple((pltpu...]
    unnamed x0 -> x6, local copies, waits for them, and re-layouts: none -> 5.35 us
where the time goes in v4:
time: 72.7 us; the launch traced here: 72.5 us
  Pallas kernels  65.9 us (91%)
  local copies, waits for them, and re-layouts  5.35 us (7%)
  between operations  1.29 us (2%)
    pallas_call x1, Pallas kernels, attention(): pl.pallas_call(functools.partial(kernel, prompts), out_shape=tuple((pltpu...  65.9 us
    unnamed x6, local copies, waits for them, and re-layouts  5.35 us

profile of v4, /device:TPU:1, one launch (start us, length us, event | category | flops | bytes accessed | tf_op | source)
XLA Modules:
  0.0 72.5 jit_solution(10893716619536157637)
XLA Ops:
  1.3 65.9 %attention.1 = (bf16[128,8192]{1,0:T(8,128)(2,1)S(1)}, bf16[128,8192]{1,0:T(8,128)(2,1)S(1)}, bf16[128,1024]{1,0:T(8,128)(2,1)S(1)}, bf16[128,1024]{1,0:T(8,128)...) custom-call(s32[1,1]{1,0:T(1,128)S(6)} %copy.25.live_ref, bf16[128,8192]{1,0:T(8,128)(2,1)} %bitcast.18, ...), custom_call_target="tpu_custom_call" | custom-call | tf_op jit(solution)/shard_map/attention/pallas_call | solution.py:445
  67.2 1.3 %copy.19 = bf16[1,1,128,8192]{3,2,1,0:T(8,128)(2,1)} copy(bf16[1,1,128,8192]{3,2,1,0:T(8,128)(2,1)S(1)} %bitcast.13) | data formatting | bytes 4194304
  68.5 1.3 %copy.20 = bf16[1,1,128,8192]{3,2,1,0:T(8,128)(2,1)} copy(bf16[1,1,128,8192]{3,2,1,0:T(8,128)(2,1)S(1)} %bitcast.12) | data formatting | bytes 4194304
  69.8 0.7 copy.23
  70.5 0.7 copy.24
  71.1 0.7 copy.21
  71.8 0.7 copy.22

commit v5 on v4

--- a/solution.py
+++ b/solution.py
@@ -489,10 +489,35 @@
     )(live, q, g, kp, vp, kr, vr)
 
 
+def write_kernel(*refs):
+    n = len(refs) // 2
+    copies = [
+        pltpu.make_async_copy(a, b, refs[2 * n].at[i])
+        for i, (a, b) in enumerate(zip(refs[:n], refs[n : 2 * n]))
+    ]
+    for copy in copies:
+        copy.start()
+    for copy in copies:
+        copy.wait()
+
+
+def write_out(*arrays):
+    return pl.pallas_call(
+        write_kernel,
+        out_shape=tuple(pltpu.HBM(a.shape, a.dtype) for a in arrays),
+        in_specs=[pl.BlockSpec(memory_space=pltpu.VMEM)] * len(arrays),
+        out_specs=(pl.BlockSpec(memory_space=pltpu.HBM),) * len(arrays),
+        scratch_shapes=[pltpu.SemaphoreType.DMA((len(arrays),))],
+        compiler_params=pltpu.CompilerParams(vmem_limit_bytes=2 * 2**20),
+        name="write_out",
+    )(*arrays)
+
+
 def shards(q, kr, vr, kp, vp, g, lengths):
     att, dq, dkr, dvr, pk, pv = attention(
         lax.axis_size("prompt"), lengths, q[0, 0], g[0, 0], kp[0], vp[0], kr[0, 0], vr[0, 0]
     )
+    att, dq, dkr, dvr, pk, pv = write_out(att, dq, dkr, dvr, pk, pv)
     return att[None, None], dq[None, None], dkr[None, None], dvr[None, None], pk[None], pv[None]
 
 

time: 72.7 us -> 69.5 us (0.956)
  local copies, waits for them, and re-layouts: 5.35 us -> 0 us
  Pallas kernels: 65.9 us -> 68.1 us
    unnamed x6 -> x0, local copies, waits for them, and re-layouts: 5.35 us -> none
    pallas_call x0 -> x1, Pallas kernels: none -> 2.29 us  [write_out(): pl.pallas_call(write_kernel, out_shape=tuple((pltpu.HBM(a.shape, a.dtype)...]
where the time goes in v5:
time: 69.5 us; the launch traced here: 69.4 us
  Pallas kernels  68.1 us (98%)
  between operations  1.29 us (2%)
    pallas_call x1, Pallas kernels, attention(): pl.pallas_call(functools.partial(kernel, prompts), out_shape=tuple((pltpu...  65.8 us
    pallas_call x1, Pallas kernels, write_out(): pl.pallas_call(write_kernel, out_shape=tuple((pltpu.HBM(a.shape, a.dtype)...  2.29 us

profile of v5, /device:TPU:1, one launch (start us, length us, event | category | flops | bytes accessed | tf_op | source)
XLA Modules:
  0.0 69.4 jit_solution(2586912773186226633)
XLA Ops:
  1.3 65.8 %attention.1 = (bf16[128,8192]{1,0:T(8,128)(2,1)S(1)}, bf16[128,8192]{1,0:T(8,128)(2,1)S(1)}, bf16[128,1024]{1,0:T(8,128)(2,1)S(1)}, bf16[128,1024]{1,0:T(8,128)...) custom-call(s32[1,1]{1,0:T(1,128)S(6)} %copy.13.live_ref, bf16[128,8192]{1,0:T(8,128)(2,1)} %bitcast.12, ...), custom_call_target="tpu_custom_call" | custom-call | tf_op jit(solution)/shard_map/attention/pallas_call | solution.py:445
  67.1 2.3 %write_out.1 = (bf16[128,8192]{1,0:T(8,128)(2,1)}, bf16[128,8192]{1,0:T(8,128)(2,1)}, bf16[128,1024]{1,0:T(8,128)(2,1)}, bf16[128,1024]{1,0:T(8,128)(2,1)}, bf16...) custom-call(bf16[128,8192]{1,0:T(8,128)(2,1)S(1)} %get-tuple-element.18.refs_0_, ...), custom_call_target="tpu_custom_call" | custom-call | tf_op jit(solution)/shard_map/write_out/pallas_call | solution.py:505
